TPU v7x, 1024 devices: a whole 8x8x8 slice. The times are simulated.
1024 devices in a mesh: rows: 64 (over y, z), feat: 16 (over x, core).
Axes of the slice: x: 8, y: 8, z: 8, core: 2. Of those that a mesh axis runs over, the one named last changes fastest.
Arguments:
- features: bfloat16 [262144, 768], P('rows', 'feat'), may hold values from -6 to 6
- w1_self: bfloat16 [768, 1024], replicated, may hold values from -0.21875 to 0.21875
- w1_neigh: bfloat16 [768, 1024], replicated, may hold values from -0.21875 to 0.21875
- bias_one: float32 [1024], replicated, may hold values from -3 to 3
- w2_self: bfloat16 [1024, 1024], replicated, may hold values from -0.1875 to 0.1875
- w2_neigh: bfloat16 [1024, 1024], replicated, may hold values from -0.1875 to 0.1875
- bias_two: float32 [1024], replicated, may hold values from -3 to 3
- owner: int32 [262144, 1], P('rows'), may hold values from 0 to 63; in each aligned block of 4096 rows (0 to 4095, 4096 to 8191, ...) at most 80 rows name the same one
- row_index: int32 [262144], P('rows'), may hold values from 0 to 4095
- count_one: int32 [16384], P('rows'), may hold values from 1 to 15
- neighbours_two: int32 [16384, 10], P(('rows', 'feat')), may hold values from 0 to 15
- count_two: int32 [16384], P(('rows', 'feat')), may hold values from 1 to 10
Outputs:
- embedding: bfloat16 [16384, 1024], P(('rows', 'feat'))
Inputs may be any that keep to these rules, and one draw needn't show every extreme that they name: Among the 4096 rows of one index of rows (aligned blocks of owner), no owner is named more than 80 times, a bound that some block reaches. `neighbours_two`: indices within the target's own block of 16 targets.
All inputs are finite; a program needn't handle non-finite values.
Results may differ from a plain program's by a relative error of at most 0.0051.
Values may be sent and summed in bfloat16 or wider, within the bound.
No kernel may reach another device: no remote copies, remote signals or barrier semaphores. Data moves between devices by JAX's collectives and lax.ppermute only.
A program may use at most 32 MiB of HBM per device.

v0:
```python
import jax
import jax.numpy as jnp
from jax import lax
from jax.sharding import PartitionSpec as P

K1 = 15
K2 = 10


def per_device(
    features,
    w1_self,
    w1_neigh,
    bias_one,
    w2_self,
    w2_neigh,
    bias_two,
    owner,
    row_index,
    count_one,
    neighbours_two,
    count_two,
):
    peers = lax.axis_size("rows")
    wanted = owner.shape[0]
    capacity = 5 * wanted // (4 * peers)
    width = features.shape[1]
    owners = owner[:, 0]
    order = jnp.argsort(owners, stable=True)
    tally = jnp.sum(
        (owners[:, None] == jnp.arange(peers, dtype=jnp.int32)[None, :]).astype(jnp.int32), axis=0
    )
    starts = jnp.cumsum(tally) - tally
    ranked = jnp.arange(wanted, dtype=jnp.int32) - starts[owners[order]]
    slots = jnp.zeros((wanted,), jnp.int32).at[order].set(ranked)
    position = owners * capacity + slots
    requests = (
        jnp.zeros((peers * capacity,), jnp.int32)
        .at[position]
        .set(row_index)
        .reshape(peers, capacity)
    )
    asked = lax.all_to_all(requests, "rows", split_axis=0, concat_axis=0, tiled=True)
    found = features[asked.reshape(-1)].reshape(asked.shape[0], asked.shape[1], width)
    replies = lax.all_to_all(found, "rows", split_axis=0, concat_axis=0, tiled=True)
    fetched = replies.reshape(peers * capacity, width)[position]
    targets = count_one.shape[0]
    grouped = fetched.reshape(targets, K1 + 1, width)
    own_rows = grouped[:, 0]
    neigh = grouped[:, 1:].astype(jnp.float32)
    valid = (jnp.arange(K1)[None, :] < count_one[:, None]).astype(jnp.float32)
    agg_one = (
        jnp.sum(neigh * valid[:, :, None], axis=1) / count_one[:, None].astype(jnp.float32)
    ).astype(jnp.bfloat16)
    offset = lax.axis_index("feat") * width
    slice_self = lax.dynamic_slice_in_dim(w1_self, offset, width, 0)
    slice_neigh = lax.dynamic_slice_in_dim(w1_neigh, offset, width, 0)
    pre_one = lax.psum_scatter(
        jnp.dot(own_rows, slice_self, preferred_element_type=jnp.float32)
        + jnp.dot(agg_one, slice_neigh, preferred_element_type=jnp.float32),
        "feat",
        scatter_dimension=0,
        tiled=True,
    )
    hidden_one = jax.nn.relu(pre_one + bias_one).astype(jnp.bfloat16)
    gathered = hidden_one[neighbours_two].astype(jnp.float32)
    valid_two = (jnp.arange(K2)[None, :] < count_two[:, None]).astype(jnp.float32)
    agg_two = (
        jnp.sum(gathered * valid_two[:, :, None], axis=1) / count_two[:, None].astype(jnp.float32)
    ).astype(jnp.bfloat16)
    total = jnp.dot(hidden_one, w2_self, preferred_element_type=jnp.float32) + jnp.dot(
        agg_two, w2_neigh, preferred_element_type=jnp.float32
    )
    return (total + bias_two).astype(jnp.bfloat16)


def solution(mesh):
    return jax.shard_map(
        per_device,
        mesh=mesh,
        in_specs=(
            P("rows", "feat"),
            P(),
            P(),
            P(),
            P(),
            P(),
            P(),
            P("rows", None),
            P("rows"),
            P("rows"),
            P(("rows", "feat"), None),
            P(("rows", "feat")),
        ),
        out_specs=P(("rows", "feat"), None),
        check_vma=False,
    )
```

profile of v0, /device:TPU:1, one launch (start us, length us, event | category | flops | bytes accessed | tf_op | source)
XLA Modules:
  0.0 295.6 jit_solution(3147114129528340257)
XLA Ops:
  6.5 1.1 convert_reduce_fusion
  7.6 0.1 copy.23
  7.7 0.1 reduce-window.9
  7.8 0.1 reduce.1
  8.0 0.7 fusion.18
  8.7 0.7 fusion.19
  9.4 0.7 fusion.16
  10.1 0.7 fusion.17
  10.8 6.5 %sort.17 = (s32[4096]{0:T(1024)}, s32[4096]{0:T(1024)S(1)}) sort(s32[4096]{0:T(1024)} %bitcast.79, s32[4096]{0:T(1024)S(1)} %iota.25), dimensions={0}, to_apply=%region_0.0 | sort | flops 49152 | bytes 65536 | tf_op jit(solution)/shard_map/jit(argsort)/sort | solution.py:29
  17.3 23.0 %gather_fusion = s32[4096]{0:T(1024)S(1)} fusion(s32[4096]{0:T(1024)S(1)} %bitcast.80, s32[4096]{0:T(1024)S(1)} %get-tuple-element.68), kind=kCustom, calls=%fused_computation | custom fusion | bytes 49152 | tf_op jit(solution)/shard_map/gather | solution.py:34
  40.4 4.3 %compare_select_fusion.2 = (s32[4096,1]{0,1:T(1,128)S(1)}, s32[4096,1]{0,1:T(1,128)S(1)}) fusion(s32[]{:T(128)} %bitcast.60, s32[]{:T(128)} %bitcast.61, s32[]{:T(128)} %bitcast.62, s32[]{:T(128)} %bitcast.63, s32[]{:T(128)} %bitcast.64, s32[]{:T(128)} %bitcast.66, s32[]{:T(128)} %bitcast.65, s32[4096,1]{0,1:T(1,128)S(1)} %bitcast.88), kind=kLoop, calls=%fused_computation.82 | loop fusion | flops 61440 | bytes 49180 | tf_op jit(solution)/shard_map/gather | solution.py:34
  44.7 2.9 compare_reduce_fusion.56
  47.6 35.9 %select_subtract_fusion = s32[4096]{0:T(1024)S(1)} fusion(pred[4096]{0:T(1024)(128)(4,1)S(1)} %get-tuple-element.63, pred[4096]{0:T(1024)(128)(4,1)S(1)} %get-tuple-element.62, pred[4096]{0:T(1024)(128)(4,1)S(1)} %get-tuple-element.61, pred[4096]{0:T(1024)(128)(4,1)S(1)} %get-tuple-element.60, pred[4096]{0:T(1024)(128)(4,1)S(1)} %get-tuple-element.59, ...), kind=kLoop, calls=%fused_computation.93 | loop fusion | flops 237568 | bytes 266468 | tf_op jit(solution)/shard_map/sub | solution.py:34
  83.5 15.5 %scatter_custom_fusion = s32[4096]{0:T(1024)S(1)} fusion(s32[4096]{0:T(1024)S(1)} %get-tuple-element.69, s32[4096]{0:T(1024)S(1)} %select_subtract_fusion, s32[]{:T(128)} %constant.10.clone.1), kind=kCustom, calls=%fused_computation.100 | custom fusion | bytes 16388 | tf_op jit(solution)/shard_map/scatter | solution.py:35
  99.1 0.6 broadcast_clamp_fusion.1
  99.7 15.7 %scatter_custom_fusion.1 = s32[5120]{0:T(1024)S(1)} fusion(s32[4096]{0:T(1024)S(1)} %get-tuple-element.65, s32[4096]{0:T(1024)} %param.20, s32[]{:T(128)} %constant.10.clone.1), kind=kCustom, calls=%fused_computation.95 | custom fusion | bytes 20992 | tf_op jit(solution)/shard_map/scatter | solution.py:40
  115.4 0.7 all_to_all.9
  116.1 24.2 %all-to-all-start = ((s32[64,1,80]{2,1,0:T(1,128)}), s32[64,1,80]{2,1,0:T(1,128)}, u32[]{:S(2)}, u32[]{:S(2)}) async-start(s32[64,1,80]{2,1,0:T(1,128)} %all_to_all.9), calls=%async_computation | async-start | bytes 65536 | tf_op jit(solution)/shard_map/all_to_all | solution.py:43
  140.4 0.5 copy.24
  140.9 10.2 %all-to-all-done = s32[64,1,80]{2,1,0:T(1,128)} async-done(((s32[64,1,80]{2,1,0:T(1,128)}), s32[64,1,80]{2,1,0:T(1,128)}, u32[]{:S(2)}, u32[]{:S(2)}) %all-to-all-start) | async-done | bytes 20512 | tf_op jit(solution)/shard_map/all_to_all | solution.py:43
  151.1 0.5 broadcast.571
  151.6 1.5 reduce.118
  153.1 0.1 reshape.136
  153.2 18.6 %gather_fusion.1 = bf16[5120,48]{1,0:T(8,128)(2,1)} fusion(bf16[4096,48]{1,0:T(8,128)(2,1)S(1)} %copy.24, s32[5120]{0:T(1024)S(1)} %broadcast_clamp_fusion), kind=kCustom, calls=%fused_computation.1 | custom fusion | bytes 1003520 | tf_op jit(solution)/shard_map/gather | solution.py:44
  171.8 2.3 copy.25
  174.2 5.6 %all-to-all-start.1 = ((bf16[64,80,48]{1,2,0:T(8,128)(2,1)}), bf16[64,80,48]{1,2,0:T(8,128)(2,1)}, u32[]{:S(2)}, u32[]{:S(2)}) async-start(bf16[64,80,48]{1,2,0:T(8,128)(2,1)} %copy.25), calls=%async_computation.1 | async-start | bytes 1572864 | tf_op jit(solution)/shard_map/all_to_all | solution.py:45
  179.8 0.2 reduce-scatter.2.cloned.1.call-start
  180.0 0.6 convert_element_type.46
  180.6 0.1 fusion.2
  180.7 19.5 %all-to-all-done.1 = bf16[64,80,48]{1,2,0:T(8,128)(2,1)} async-done(((bf16[64,80,48]{1,2,0:T(8,128)(2,1)}), bf16[64,80,48]{1,2,0:T(8,128)(2,1)}, u32[]{:S(2)}, u32[]{:S(2)}) %all-to-all-start.1) | async-done | bytes 491552 | tf_op jit(solution)/shard_map/all_to_all | solution.py:45
  200.2 1.6 copy.26
  201.9 14.9 %gather_fusion.2 = bf16[4096,48]{1,0:T(8,128)(2,1)} fusion(bf16[5120,48]{1,0:T(8,128)(2,1)S(1)} %bitcast.82, s32[4096]{0:T(1024)S(1)} %copy-done.4), kind=kCustom, calls=%fused_computation.2 | custom fusion | bytes 802816 | tf_op jit(solution)/shard_map/gather | solution.py:46
  216.8 1.1 slice.81
  217.9 0.1 copy.28
  218.0 2.5 multiply_reduce_fusion
  220.5 1.2 fusion.4
  221.8 2.2 convolution_add_fusion
  224.0 0.0 reduce-scatter.2.cloned.1.call-update
  224.0 0.1 reshape.237
  224.2 0.1 fusion.13
  224.2 60.0 %reduce-scatter.2.cloned.1.call-done = f32[16,1024]{1,0:T(8,128)} async-done(((f32[256,1024]{1,0:T(8,128)}), f32[16,1024]{1,0:T(8,128)}) %reduce-scatter.2.cloned.1.call-update) | async-done | bytes 65552 | tf_op jit(solution)/shard_map/reduce_scatter | solution.py:58
  284.3 0.8 maximum_convert_fusion
  285.1 0.9 gather_fusion.3
  286.0 0.1 reshape.265
  286.2 0.4 fusion.20
  286.6 0.3 multiply_reduce_fusion.1
  286.8 0.9 copy-done.2
  287.7 1.0 fusion.1
  (29 shorter events, 0.1 us)
Async XLA Ops:
  6.5 279.6 %copy-start = (bf16[1024,1024]{1,0:T(8,128)(2,1)S(1)}, bf16[1024,1024]{1,0:T(8,128)(2,1)}, u32[]{:S(2)}) copy-start(bf16[1024,1024]{1,0:T(8,128)(2,1)} %param.16) | copy-start | bytes 6291460
  6.5 10.8 %copy-start.1 = (s32[4096,1]{0,1:T(1,128)S(1)}, s32[4096,1]{0,1:T(1,128)}, u32[]{:S(2)}) copy-start(s32[4096,1]{0,1:T(1,128)} %param.19) | copy-start | bytes 49156
  17.3 123.0 %copy-start.3 = (bf16[4096,48]{0,1:T(8,128)(2,1)S(1)}, bf16[4096,48]{0,1:T(8,128)(2,1)}, u32[]{:S(2)}) copy-start(bf16[4096,48]{0,1:T(8,128)(2,1)} %param.12) | copy-start | bytes 1179652
  116.1 34.9 %all-to-all-start = ((s32[64,1,80]{2,1,0:T(1,128)}), s32[64,1,80]{2,1,0:T(1,128)}, u32[]{:S(2)}, u32[]{:S(2)}) async-start(s32[64,1,80]{2,1,0:T(1,128)} %all_to_all.9), calls=%async_computation | async-start | bytes 65536 | tf_op jit(solution)/shard_map/all_to_all | solution.py:43
  171.8 8.2 %copy-start.7 = (s32[256]{0:T(256)S(1)}, s32[256]{0:T(256)}, u32[]{:S(2)}) copy-start(s32[256]{0:T(256)} %param.21) | copy-start | bytes 3076
  174.2 27.7 %copy-start.4 = (s32[4096]{0:T(1024)S(1)}, s32[4096]{0:T(1024)}, u32[]{:S(2)}) copy-start(s32[4096]{0:T(1024)} %get-tuple-element.64) | copy-start | bytes 49156
  174.2 26.1 %all-to-all-start.1 = ((bf16[64,80,48]{1,2,0:T(8,128)(2,1)}), bf16[64,80,48]{1,2,0:T(8,128)(2,1)}, u32[]{:S(2)}, u32[]{:S(2)}) async-start(bf16[64,80,48]{1,2,0:T(8,128)(2,1)} %copy.25), calls=%async_computation.1 | async-start | bytes 1572864 | tf_op jit(solution)/shard_map/all_to_all | solution.py:45
  179.8 104.5 %reduce-scatter.2.cloned.1.call-start = ((), (), s32[]{:S(2)}) async-start(), calls=%async_computation.3 | async-start | bytes 1114112 | tf_op jit(solution)/shard_map/reduce_scatter | solution.py:58
  216.8 4.9 %copy-start.8 = (f32[256]{0:T(256)S(1)}, f32[256]{0:T(256)}, u32[]{:S(2)}) copy-start(f32[256]{0:T(256)} %convert_element_type.46) | copy-start | bytes 3076
  221.7 2.3 copy-start.5
  221.7 2.4 copy-start.10
  221.7 62.5 %copy-start.9 = (f32[1024]{0:T(1024)S(1)}, f32[1024]{0:T(1024)}, u32[]{:S(2)}) copy-start(f32[1024]{0:T(1024)} %param.15) | copy-start | bytes 12292
  286.2 1.6 copy-start.2
  286.2 1.6 copy-start.6
Sparse Core Ops, SparseCore 0:
  224.1 60.0 reduce-scatter.1
where the time goes:
time: 297 us; the launch traced here: 296 us
  local copies, waits for them, and re-layouts  99.8 us (34%)
  waiting for transfers between devices  89.8 us (30%)
  other arithmetic  57.4 us (19%)
  starting transfers between devices  30 us (10%)
  between operations  13.7 us (5%)
  matrix products  4.88 us (2%)
    reduce_scatter x1, waiting for transfers between devices, per_device(): lax.psum_scatter(jnp.dot(own_rows, slice_self, preferred_element_type=jnp...  60 us
    sub x1, other arithmetic, per_device(): ranked = jnp.arange(wanted, dtype=jnp.int32) - starts[owners[order]]  35.9 us
    gather x5, local copies, waits for them, and re-layouts, per_device(): ranked = jnp.arange(wanted, dtype=jnp.int32) - starts[owners[order]]  25.9 us
    all_to_all x1, starting transfers between devices, per_device(): lax.all_to_all(requests, 'rows', split_axis=0, concat_axis=0, tiled=True)  24.2 us
    all_to_all x1, waiting for transfers between devices, per_device(): lax.all_to_all(found, 'rows', split_axis=0, concat_axis=0, tiled=True)  19.5 us
    gather x1, local copies, waits for them, and re-layouts, per_device(): features[asked.reshape(-1)].reshape(asked.shape[0], asked.shape[1], width)  18.6 us
    scatter x1, local copies, waits for them, and re-layouts, per_device(): requests = jnp.zeros((peers * capacity,), jnp.int32).at[position].set(row...  15.7 us
    scatter x1, local copies, waits for them, and re-layouts, per_device(): slots = jnp.zeros((wanted,), jnp.int32).at[order].set(ranked)  15.5 us
  transfers between devices with their start and end apart: 3, of which 3 were waited for; matrix products, arithmetic and copies ran while one was open for 0% of the time, Pallas kernels for 0%

commit v1 on v0

v1 whole, which is shorter than its diff:
```python
import jax
import jax.numpy as jnp
from jax import lax
from jax.experimental import pallas as pl
from jax.experimental.pallas import tpu as pltpu
from jax.sharding import PartitionSpec as P

K1 = 15
K2 = 10
LANES = 128
PEERS = 64
CAPACITY = 80
HALF = CAPACITY // 2
GROUPS = 3
WIDTH = 48
PART = WIDTH // GROUPS
TRIPLES = -(-PEERS // GROUPS)
HIGH = 256
LOWS = 16
BLOCK = 16
VMEM = pltpu.VMEM
LIMIT = 48 * 1024 * 1024
NT = (((1,), (1,)), ((), ()))


def iota(shape, dimension):
    return lax.broadcasted_iota(jnp.int32, shape, dimension)


def route_kernel(owner_ref, row_ref, count_ref, request_ref, code_ref):
    chunks = owner_ref.shape[0]
    mask = owner_ref[...][:, None, :] == iota((chunks, PEERS, LANES), 1)
    ones = jnp.where(mask, 1.0, 0.0)
    before = iota((LANES, 2 * LANES), 0)
    upto = iota((LANES, 2 * LANES), 1)
    prefix = jnp.where((before < upto) | (upto >= LANES), 1.0, 0.0).astype(jnp.bfloat16)
    sums = jnp.dot(
        ones.astype(jnp.bfloat16).reshape(chunks * PEERS, LANES),
        prefix,
        preferred_element_type=jnp.float32,
    ).reshape(chunks, PEERS, 2 * LANES)

    per_chunk = LANES // (K1 + 1)
    half = chunks // 2
    chunk = iota((chunks, LANES), 0)
    lane = iota((chunks, LANES), 1)
    count = count_ref[...].astype(jnp.float32)
    spread = jnp.concatenate(
        [jnp.broadcast_to(count[i : i + 1], (half, LANES)) for i in range(2)], axis=0
    )
    spread = jnp.where(lane // per_chunk == chunk % half, spread, 0.0)
    pick = jnp.where(
        iota((LANES, LANES), 0) % per_chunk == iota((LANES, LANES), 1) // (K1 + 1), 1.0, 0.0
    )
    limit = jnp.dot(
        spread.astype(jnp.bfloat16), pick.astype(jnp.bfloat16), preferred_element_type=jnp.float32
    )
    place = lane % (K1 + 1)
    target = (chunk * per_chunk + lane // (K1 + 1) + 1).astype(jnp.float32)
    code = jnp.where(
        place == 0, -target, jnp.where(place.astype(jnp.float32) <= limit, target, 0.0)
    )
    row = row_ref[...]
    high = (row >> 6).astype(jnp.float32)
    low = (row & 63).astype(jnp.float32)

    offset = jnp.zeros((PEERS, LANES), jnp.float32)
    total = jnp.zeros((3 * PEERS, CAPACITY), jnp.float32)
    slot = iota((CAPACITY, LANES), 0).astype(jnp.float32)
    values, slots = [], []
    for c in range(chunks):
        here = mask[c]
        rank = jnp.sum(
            jnp.where(here, sums[c, :, :LANES] + offset, 0.0), axis=0, keepdims=True
        )
        offset = offset + sums[c, :, LANES:]
        slots.append(jnp.where(slot == rank, 1.0, 0.0).astype(jnp.bfloat16))
        values.append(
            jnp.concatenate(
                [jnp.where(here, v[c : c + 1], 0.0) for v in (high, low, code)], axis=0
            ).astype(jnp.bfloat16)
        )
        if c % 2 == 1:
            total = total + lax.dot_general(
                jnp.concatenate(values, axis=1),
                jnp.concatenate(slots, axis=1),
                NT,
                preferred_element_type=jnp.float32,
            )
            values, slots = [], []
    request_ref[...] = jnp.zeros_like(request_ref)
    code_ref[...] = jnp.zeros_like(code_ref)
    request_ref[:, 0, :CAPACITY] = (
        total[:PEERS] * 64.0 + total[PEERS : 2 * PEERS]
    ).astype(jnp.int32)
    code_ref[:, :CAPACITY] = total[2 * PEERS :]


def spread_halves(slots, scratch):
    lane = iota(slots.shape, 1)

    def pick(parts):
        out = jnp.where(lane < HALF, parts[0], jnp.where(lane < 2 * HALF, parts[1], parts[2]))
        return jnp.where(lane < GROUPS * HALF, out, jnp.zeros_like(out))

    scratch[:, PEERS:, :] = jnp.zeros_like(scratch[:, PEERS:, :])
    scratch[0, :PEERS, :] = pick([slots, pltpu.roll(slots, HALF, 1), pltpu.roll(slots, 2 * HALF, 1)])
    scratch[1, :PEERS, :] = pick([pltpu.roll(slots, LANES - HALF, 1), slots, pltpu.roll(slots, HALF, 1)])


def triple_row(scratch, half, triple):
    lane = iota((1, LANES), 1)
    rows = [scratch[half, pl.ds(GROUPS * triple + x, 1), :] for x in range(GROUPS)]
    return jnp.where(lane < HALF, rows[0], jnp.where(lane < 2 * HALF, rows[1], rows[2]))


def swap_groups(parts):
    lane = iota(parts[0].shape, 1)
    out = []
    for x in range(GROUPS):
        moved = [
            parts[b] if b == x else pltpu.roll(parts[b], (HALF * (b - x)) % LANES, 1)
            for b in range(GROUPS)
        ]
        out.append(
            jnp.where(lane < HALF, moved[0], jnp.where(lane < 2 * HALF, moved[1], moved[2]))
        )
    return out


def find_kernel(asked_ref, features_ref, found_ref, table, scratch):
    spread_halves(asked_ref[:, 0, :], scratch)
    for low in range(LOWS):
        table[low * WIDTH : (low + 1) * WIDTH, :] = features_ref[:, low * HIGH : (low + 1) * HIGH]

    def step(triple, last):
        index = jnp.concatenate([triple_row(scratch, h, triple) for h in range(2)], axis=1)
        chosen = jnp.where(iota((HIGH, 2 * LANES), 0) == (index & (HIGH - 1)), 1.0, 0.0)
        rows = jnp.dot(table[...], chosen.astype(jnp.bfloat16), preferred_element_type=jnp.float32)
        low = index >> 8
        out = jnp.zeros((WIDTH, 2 * LANES), jnp.float32)
        for k in range(LOWS):
            out = jnp.where(low == k, rows[k * WIDTH : (k + 1) * WIDTH], out)
        for h in range(2):
            half = out[:, h * LANES : (h + 1) * LANES]
            tiles = swap_groups([half[b * PART : (b + 1) * PART] for b in range(GROUPS)])
            for x in range(1 if last else GROUPS):
                found_ref[GROUPS * triple + x, h * PART : (h + 1) * PART, :] = tiles[x].astype(
                    jnp.bfloat16
                )

    def body(i, carry):
        for k in range(3):
            step(3 * i + k, False)
        return carry

    lax.fori_loop(0, (TRIPLES - 1) // 3, body, 0)
    step(TRIPLES - 1, True)


def mean_kernel(reply_ref, code_ref, out_ref, scratch, total):
    spread_halves(code_ref[...], scratch)
    targets = out_ref.shape[0]
    total[...] = jnp.zeros_like(total)

    def step(triple, last):
        code = jnp.concatenate([triple_row(scratch, h, triple) for h in range(2)], axis=1)
        row = iota((2 * targets, 2 * LANES), 0)
        wanted = jnp.where(row < targets, -(row + 1), row - targets + 1).astype(jnp.float32)
        member = jnp.where(wanted == code, 1.0, 0.0).astype(jnp.bfloat16)
        halves = []
        for h in range(2):
            tiles = [
                reply_ref[
                    GROUPS * triple + (0 if last else x), h * PART : (h + 1) * PART, :
                ].astype(jnp.float32)
                for x in range(GROUPS)
            ]
            columns = swap_groups(tiles)
            halves.append(
                jnp.concatenate(
                    columns + columns + [jnp.ones((2 * PART, LANES), jnp.float32)], axis=0
                ).astype(jnp.bfloat16)
            )
        total[...] += lax.dot_general(
            member, jnp.concatenate(halves, axis=1), NT, preferred_element_type=jnp.float32
        )

    def body(i, carry):
        for k in range(3):
            step(3 * i + k, False)
        return carry

    lax.fori_loop(0, (TRIPLES - 1) // 3, body, 0)
    step(TRIPLES - 1, True)
    own = total[:targets]
    neigh = total[targets:]
    mean = neigh / neigh[:, 2 * WIDTH : 2 * WIDTH + 1]
    out_ref[...] = jnp.where(iota(own.shape, 1) < WIDTH, own, mean).astype(jnp.bfloat16)


def layers_kernel(
    part_ref,
    w1_self_ref,
    w1_neigh_ref,
    bias_one_ref,
    w2_self_ref,
    w2_neigh_ref,
    bias_two_ref,
    neighbours_ref,
    count_ref,
    out_ref,
):
    parts = [part_ref[i].astype(jnp.float32) for i in range(part_ref.shape[0])]
    own = jnp.concatenate([p[:, :WIDTH] for p in parts], axis=1).astype(jnp.bfloat16)
    mean = jnp.concatenate([p[:, WIDTH : 2 * WIDTH] for p in parts], axis=1).astype(jnp.bfloat16)
    pre = jnp.dot(own, w1_self_ref[...], preferred_element_type=jnp.float32) + jnp.dot(
        mean, w1_neigh_ref[...], preferred_element_type=jnp.float32
    )
    hidden = jnp.maximum(pre + bias_one_ref[...], 0.0).astype(jnp.bfloat16)
    lane = iota((BLOCK, BLOCK), 1)
    count = jnp.sum(
        jnp.where(lane == iota((BLOCK, BLOCK), 0), count_ref[...].astype(jnp.float32), 0.0),
        axis=1,
        keepdims=True,
    )
    member = jnp.zeros((BLOCK, BLOCK), jnp.float32)
    for j in range(K2):
        named = (neighbours_ref[:, j : j + 1] == lane) & (count > j)
        member = member + jnp.where(named, 1.0, 0.0)
    sums = jnp.dot(member.astype(jnp.bfloat16), hidden, preferred_element_type=jnp.float32)
    mean_two = (sums / count).astype(jnp.bfloat16)
    total = jnp.dot(hidden, w2_self_ref[...], preferred_element_type=jnp.float32) + jnp.dot(
        mean_two, w2_neigh_ref[...], preferred_element_type=jnp.float32
    )
    out_ref[...] = (total + bias_two_ref[...]).astype(jnp.bfloat16)


def call(kernel, out_shape, scratch_shapes, *operands):
    return pl.pallas_call(
        kernel,
        out_shape=out_shape,
        in_specs=[pl.BlockSpec(memory_space=VMEM)] * len(operands),
        out_specs=jax.tree.map(lambda _: pl.BlockSpec(memory_space=VMEM), out_shape),
        scratch_shapes=scratch_shapes,
        compiler_params=pltpu.CompilerParams(vmem_limit_bytes=LIMIT),
    )(*operands)


def route(owner, row_index, count_one):
    lines = owner.shape[0] // LANES
    return call(
        route_kernel,
        [
            jax.ShapeDtypeStruct((PEERS, 1, LANES), jnp.int32),
            jax.ShapeDtypeStruct((PEERS, LANES), jnp.float32),
        ],
        [],
        owner.reshape(lines, LANES),
        row_index.reshape(lines, LANES),
        count_one.reshape(-1, LANES),
    )


def find(asked, features):
    return call(
        find_kernel,
        jax.ShapeDtypeStruct((PEERS, 2 * PART, LANES), jnp.bfloat16),
        [
            pltpu.VMEM((LOWS * WIDTH, HIGH), jnp.bfloat16),
            pltpu.VMEM((2, PEERS + 8, LANES), jnp.int32),
        ],
        asked,
        features.T,
    )


def means(replies, code, targets):
    return call(
        mean_kernel,
        jax.ShapeDtypeStruct((targets, LANES), jnp.bfloat16),
        [
            pltpu.VMEM((2, PEERS + 8, LANES), jnp.float32),
            pltpu.VMEM((2 * targets, LANES), jnp.float32),
        ],
        replies,
        code,
    )


def layers(parts, w1_self, w1_neigh, bias_one, w2_self, w2_neigh, bias_two, neighbours, count):
    return call(
        layers_kernel,
        jax.ShapeDtypeStruct((BLOCK, w2_self.shape[1]), jnp.bfloat16),
        [],
        parts,
        w1_self,
        w1_neigh,
        bias_one.reshape(1, -1),
        w2_self,
        w2_neigh,
        bias_two.reshape(1, -1),
        neighbours,
        count.reshape(1, -1),
    )


def per_device(
    features,
    w1_self,
    w1_neigh,
    bias_one,
    w2_self,
    w2_neigh,
    bias_two,
    owner,
    row_index,
    count_one,
    neighbours_two,
    count_two,
):
    requests, code = route(owner, row_index, count_one)
    asked = lax.all_to_all(requests, "rows", split_axis=0, concat_axis=0, tiled=True)
    found = find(asked, features)
    replies = lax.all_to_all(found, "rows", split_axis=0, concat_axis=0, tiled=True)
    mine = means(replies, code, count_one.shape[0])
    mine = mine.reshape(-1, BLOCK, LANES)
    parts = lax.all_to_all(mine, "feat", split_axis=0, concat_axis=0, tiled=True)
    return layers(
        parts, w1_self, w1_neigh, bias_one, w2_self, w2_neigh, bias_two, neighbours_two, count_two
    )


def solution(mesh):
    return jax.shard_map(
        per_device,
        mesh=mesh,
        in_specs=(
            P("rows", "feat"),
            P(),
            P(),
            P(),
            P(),
            P(),
            P(),
            P("rows", None),
            P("rows"),
            P("rows"),
            P(("rows", "feat"), None),
            P(("rows", "feat")),
        ),
        out_specs=P(("rows", "feat"), None),
        check_vma=False,
    )
```

time: 297 us -> 92.6 us (0.31)
  local copies, waits for them, and re-layouts: 99.8 us -> 6.09 us
  waiting for transfers between devices: 89.8 us -> 0 us
  blocking collectives: 0 us -> 73.2 us
  other arithmetic: 57.4 us -> 0 us
  starting transfers between devices: 30 us -> 0 us
  between operations: 13.7 us -> 0.05 us
  Pallas kernels: 0 us -> 12.9 us
  matrix products: 4.88 us -> 0 us
    all_to_all x0 -> x3, blocking collectives: none -> 73.2 us  [the longest x1 34.6 us: per_device(): lax.all_to_all(requests, 'rows', split_axis=0, concat_axis=0, tiled=True)]
    gather x8 -> x0, local copies, waits for them, and re-layouts: 60.3 us -> none  [the longest x5 25.9 us: per_device(): ranked = jnp.arange(wanted, dtype=jnp.int32) - starts[owners[order]]]
    reduce_scatter x1 -> x0, waiting for transfers between devices: 60 us -> none  [per_device(): lax.psum_scatter(jnp.dot(own_rows, slice_self, preferred_element_type=jnp...]
    sub x2 -> x0, other arithmetic: 35.9 us -> none  [the longest x1 35.9 us: per_device(): ranked = jnp.arange(wanted, dtype=jnp.int32) - starts[owners[order]]]
    scatter x2 -> x0, local copies, waits for them, and re-layouts: 31.2 us -> none  [the longest x1 15.7 us: per_device(): requests = jnp.zeros((peers * capacity,), jnp.int32).at[position].set(row...]
    all_to_all x2 -> x0, starting transfers between devices: 29.8 us -> none  [the longest x1 24.2 us: per_device(): lax.all_to_all(requests, 'rows', split_axis=0, concat_axis=0, tiled=True)]
    all_to_all x2 -> x0, waiting for transfers between devices: 29.7 us -> none  [the longest x1 19.5 us: per_device(): lax.all_to_all(found, 'rows', split_axis=0, concat_axis=0, tiled=True)]
    pallas_call x0 -> x4, Pallas kernels: none -> 12.9 us  [call(): pl.pallas_call(kernel, out_shape=out_shape, in_specs=[pl.BlockSpec(memory...]
  transfers between devices with their start and end apart: 3 -> 0, of which waited for: 3 -> 0; matrix products, arithmetic and copies ran while one was open for 0% -> 0% of each run, Pallas kernels for 0% -> 0%
where the time goes in v1:
time: 92.6 us; the launch traced here: 92.2 us
  blocking collectives  73.2 us (79%)
  Pallas kernels  12.9 us (14%)
  local copies, waits for them, and re-layouts  6.09 us (7%)
    all_to_all x1, blocking collectives, per_device(): lax.all_to_all(requests, 'rows', split_axis=0, concat_axis=0, tiled=True)  34.6 us
    all_to_all x1, blocking collectives, per_device(): lax.all_to_all(mine, 'feat', split_axis=0, concat_axis=0, tiled=True)  19.4 us
    all_to_all x1, blocking collectives, per_device(): lax.all_to_all(found, 'rows', split_axis=0, concat_axis=0, tiled=True)  19.2 us
    pallas_call x4, Pallas kernels, call(): pl.pallas_call(kernel, out_shape=out_shape, in_specs=[pl.BlockSpec(memory...  12.9 us
    unnamed x22, local copies, waits for them, and re-layouts  6.09 us

profile of v1, /device:TPU:1, one launch (start us, length us, event | category | flops | bytes accessed | tf_op | source)
XLA Modules:
  0.0 92.2 jit_solution(11579302846488662019)
XLA Ops:
  0.0 0.0 copy-start
  0.0 0.0 copy-start.4
  0.0 0.9 copy-done.4
  0.9 0.0 copy-start.5
  0.9 0.7 copy-done.5
  1.6 0.0 copy-start.9
  1.6 0.7 copy-done.9
  2.3 1.0 %shard_map.118 = (s32[64,1,128]{2,1,0:T(1,128)S(1)}, f32[64,128]{1,0:T(8,128)S(1)}) custom-call(s32[32,128]{1,0:T(8,128)S(1)} %bitcast.10, s32[32,128]{1,0:T(8,128)S(1)} %bitcast.11, s32[2,128]{1,0:T(2,128)S(1)} %bitcast.14), custom_call_target="tpu_custom_call" | custom-call | tf_op jit(solution)/shard_map/pallas_call | solution.py:240
  3.3 34.6 %all_to_all.15.asked_ref = s32[64,1,128]{2,1,0:T(1,128)S(1)} all-to-all(s32[64,1,128]{2,1,0:T(1,128)S(1)} %get-tuple-element.7), channel_id=1, replica_groups=mesh['rows'=64,'feat'=16] {'rows'}, dimensions={0} | all-to-all | bytes 65536 | tf_op jit(solution)/shard_map/all_to_all | solution.py:323
  37.9 0.0 copy-start.3
  37.9 1.0 %copy-done.3 = bf16[4096,48]{0,1:T(8,128)(2,1)S(1)} copy-done((bf16[4096,48]{0,1:T(8,128)(2,1)S(1)}, bf16[4096,48]{0,1:T(8,128)(2,1)}, u32[]{:S(2)}) %copy-start.3) | copy-done | bytes 393240
  38.9 0.0 copy-start.6
  38.9 0.0 copy-start.7
  38.9 0.0 copy-start.8
  38.9 0.0 copy-start.10
  38.9 4.7 %shard_map.119 = bf16[64,32,128]{2,1,0:T(8,128)(2,1)S(1)} custom-call(s32[64,1,128]{2,1,0:T(1,128)S(1)} %all_to_all.15.asked_ref, bf16[48,4096]{1,0:T(8,128)(2,1)S(1)} %bitcast.8), custom_call_target="tpu_custom_call" | custom-call | tf_op jit(solution)/shard_map/pallas_call | solution.py:240
  43.6 19.2 %all_to_all.16.reply_ref = bf16[64,32,128]{2,1,0:T(8,128)(2,1)S(1)} all-to-all(bf16[64,32,128]{2,1,0:T(8,128)(2,1)S(1)} %shard_map.119), channel_id=1, replica_groups=mesh['rows'=64,'feat'=16] {'rows'}, dimensions={0} | all-to-all | bytes 1048576 | tf_op jit(solution)/shard_map/all_to_all | solution.py:325
  62.8 3.7 %shard_map.120 = bf16[256,128]{1,0:T(8,128)(2,1)S(1)} custom-call(bf16[64,32,128]{2,1,0:T(8,128)(2,1)S(1)} %all_to_all.16.reply_ref, f32[64,128]{1,0:T(8,128)S(1)} %get-tuple-element.8.code_ref), custom_call_target="tpu_custom_call" | custom-call | tf_op jit(solution)/shard_map/pallas_call | solution.py:240
  66.5 19.4 %all_to_all.17.part_ref = bf16[16,16,128]{2,1,0:T(8,128)(2,1)S(1)} all-to-all(bf16[16,16,128]{2,1,0:T(8,128)(2,1)S(1)} %bitcast.9), channel_id=1, replica_groups=mesh['rows'=64,'feat'=16] {'feat'}, dimensions={0} | all-to-all | bytes 131072 | tf_op jit(solution)/shard_map/all_to_all | solution.py:328
  85.9 0.0 copy-done
  85.9 0.0 copy-done.6
  85.9 0.0 copy-done.7
  85.9 0.0 copy-done.8
  85.9 0.0 copy-done.10
  85.9 0.0 copy-start.1
  85.9 1.4 %copy-done.1 = bf16[768,1024]{1,0:T(8,128)(2,1)S(1)} copy-done((bf16[768,1024]{1,0:T(8,128)(2,1)S(1)}, bf16[768,1024]{1,0:T(8,128)(2,1)}, u32[]{:S(2)}) %copy-start.1) | copy-done | bytes 1572888
  87.3 0.0 copy-start.2
  87.3 1.4 %copy-done.2 = bf16[768,1024]{1,0:T(8,128)(2,1)S(1)} copy-done((bf16[768,1024]{1,0:T(8,128)(2,1)S(1)}, bf16[768,1024]{1,0:T(8,128)(2,1)}, u32[]{:S(2)}) %copy-start.2) | copy-done | bytes 1572888
  88.7 3.5 %shard_map.121 = bf16[16,1024]{1,0:T(8,128)(2,1)} custom-call(bf16[16,16,128]{2,1,0:T(8,128)(2,1)S(1)} %all_to_all.17.part_ref, bf16[768,1024]{1,0:T(8,128)(2,1)S(1)} %copy-done.1, bf16[768,1024]{1,0:T(8,128)(2,1)S(1)} %copy-done.2, f32[1,1024]{1,0:T(1,128)S(1)} %bitcast.12, bf16[1024,1024]{1,0:T(8,128)(2,1)S(1)} %copy-done, ...), custom_call_target="tpu_custom_call" | custom-call | tf_op jit(solution)/shard_map/pallas_call | solution.py:240
Async XLA Ops:
  0.0 85.9 %copy-start = (bf16[1024,1024]{1,0:T(8,128)(2,1)S(1)}, bf16[1024,1024]{1,0:T(8,128)(2,1)}, u32[]{:S(2)}) copy-start(bf16[1024,1024]{1,0:T(8,128)(2,1)} %w2_self_ref.1) | copy-start | bytes 6291460
  0.0 0.9 copy-start.4
  0.9 0.7 copy-start.5
  1.6 0.7 copy-start.9
  37.9 1.0 %copy-start.3 = (bf16[4096,48]{0,1:T(8,128)(2,1)S(1)}, bf16[4096,48]{0,1:T(8,128)(2,1)}, u32[]{:S(2)}) copy-start(bf16[4096,48]{0,1:T(8,128)(2,1)} %param.12) | copy-start | bytes 1179652
  38.9 47.0 %copy-start.6 = (s32[16,10]{1,0:T(8,128)S(1)}, s32[16,10]{1,0:T(8,128)}, u32[]{:S(2)}) copy-start(s32[16,10]{1,0:T(8,128)} %neighbours_ref.1) | copy-start | bytes 1924
  38.9 47.0 %copy-start.7 = (f32[1024]{0:T(1024)S(1)}, f32[1024]{0:T(1024)}, u32[]{:S(2)}) copy-start(f32[1024]{0:T(1024)} %param.15) | copy-start | bytes 12292
  38.9 47.0 %copy-start.8 = (f32[1024]{0:T(1024)S(1)}, f32[1024]{0:T(1024)}, u32[]{:S(2)}) copy-start(f32[1024]{0:T(1024)} %param.18) | copy-start | bytes 12292
  38.9 47.0 %copy-start.10 = (s32[16]{0:T(128)S(1)}, s32[16]{0:T(128)}, u32[]{:S(2)}) copy-start(s32[16]{0:T(128)} %param.23) | copy-start | bytes 196
  85.9 1.4 %copy-start.1 = (bf16[768,1024]{1,0:T(8,128)(2,1)S(1)}, bf16[768,1024]{1,0:T(8,128)(2,1)}, u32[]{:S(2)}) copy-start(bf16[768,1024]{1,0:T(8,128)(2,1)} %w1_self_ref.1) | copy-start | bytes 4718596
  87.3 1.4 %copy-start.2 = (bf16[768,1024]{1,0:T(8,128)(2,1)S(1)}, bf16[768,1024]{1,0:T(8,128)(2,1)}, u32[]{:S(2)}) copy-start(bf16[768,1024]{1,0:T(8,128)(2,1)} %w1_neigh_ref.1) | copy-start | bytes 4718596

commit v2 on v1

--- a/solution.py
+++ b/solution.py
@@ -19,7 +19,7 @@
 LOWS = 16
 BLOCK = 16
 VMEM = pltpu.VMEM
-LIMIT = 48 * 1024 * 1024
+LIMIT = 12 * 1024 * 1024
 NT = (((1,), (1,)), ((), ()))
 
 
@@ -27,7 +27,19 @@
     return lax.broadcasted_iota(jnp.int32, shape, dimension)
 
 
-def route_kernel(owner_ref, row_ref, count_ref, request_ref, code_ref):
+def route_kernel(
+    owner_hbm, row_hbm, count_hbm, request_ref, code_ref, owner_ref, row_ref, count_ref, arrived
+):
+    copies = [
+        pltpu.make_async_copy(source, target, arrived.at[i])
+        for i, (source, target) in enumerate(
+            ((owner_hbm, owner_ref), (row_hbm, row_ref), (count_hbm, count_ref))
+        )
+    ]
+    for copy in copies:
+        copy.start()
+    for copy in copies:
+        copy.wait()
     chunks = owner_ref.shape[0]
     mask = owner_ref[...][:, None, :] == iota((chunks, PEERS, LANES), 1)
     ones = jnp.where(mask, 1.0, 0.0)
@@ -236,14 +248,15 @@
     out_ref[...] = (total + bias_two_ref[...]).astype(jnp.bfloat16)
 
 
-def call(kernel, out_shape, scratch_shapes, *operands):
+def call(kernel, out_shape, scratch_shapes, flops, *operands, space=VMEM):
     return pl.pallas_call(
         kernel,
         out_shape=out_shape,
-        in_specs=[pl.BlockSpec(memory_space=VMEM)] * len(operands),
+        in_specs=[pl.BlockSpec(memory_space=space)] * len(operands),
         out_specs=jax.tree.map(lambda _: pl.BlockSpec(memory_space=VMEM), out_shape),
         scratch_shapes=scratch_shapes,
         compiler_params=pltpu.CompilerParams(vmem_limit_bytes=LIMIT),
+        cost_estimate=pl.CostEstimate(flops=flops, bytes_accessed=1 << 20, transcendentals=0),
     )(*operands)
 
 
@@ -255,10 +268,18 @@
             jax.ShapeDtypeStruct((PEERS, 1, LANES), jnp.int32),
             jax.ShapeDtypeStruct((PEERS, LANES), jnp.float32),
         ],
-        [],
-        owner.reshape(lines, LANES),
-        row_index.reshape(lines, LANES),
-        count_one.reshape(-1, LANES),
+        [
+            pltpu.VMEM((lines, LANES), jnp.int32),
+            pltpu.VMEM((lines, LANES), jnp.int32),
+            pltpu.VMEM((count_one.shape[0] // LANES, LANES), jnp.int32),
+            pltpu.SemaphoreType.DMA((3,)),
+        ],
+        1 << 30,
+        *[
+            pltpu.with_memory_space_constraint(a.reshape(-1, LANES), pltpu.HBM)
+            for a in (owner, row_index, count_one)
+        ],
+        space=pltpu.HBM,
     )
 
 
@@ -270,6 +291,7 @@
             pltpu.VMEM((LOWS * WIDTH, HIGH), jnp.bfloat16),
             pltpu.VMEM((2, PEERS + 8, LANES), jnp.int32),
         ],
+        5 << 30,
         asked,
         features.T,
     )
@@ -283,6 +305,7 @@
             pltpu.VMEM((2, PEERS + 8, LANES), jnp.float32),
             pltpu.VMEM((2 * targets, LANES), jnp.float32),
         ],
+        4 << 30,
         replies,
         code,
     )
@@ -293,6 +316,7 @@
         layers_kernel,
         jax.ShapeDtypeStruct((BLOCK, w2_self.shape[1]), jnp.bfloat16),
         [],
+        3 << 30,
         parts,
         w1_self,
         w1_neigh,

time: 92.6 us -> 85.7 us (0.925)
  local copies, waits for them, and re-layouts: 6.09 us -> 0.04 us
    unnamed x22 -> x18, local copies, waits for them, and re-layouts: 6.09 us -> 0.04 us
where the time goes in v2:
time: 85.7 us; the launch traced here: 85.5 us
  blocking collectives  73.2 us (85%)
  Pallas kernels  12.1 us (14%)
    all_to_all x1, blocking collectives, per_device(): lax.all_to_all(requests, 'rows', split_axis=0, concat_axis=0, tiled=True)  34.6 us
    all_to_all x1, blocking collectives, per_device(): lax.all_to_all(mine, 'feat', split_axis=0, concat_axis=0, tiled=True)  19.4 us
    all_to_all x1, blocking collectives, per_device(): lax.all_to_all(found, 'rows', split_axis=0, concat_axis=0, tiled=True)  19.2 us
    pallas_call x4, Pallas kernels, call(): pl.pallas_call(kernel, out_shape=out_shape, in_specs=[pl.BlockSpec(memory...  12.1 us

profile of v2, /device:TPU:1, one launch (start us, length us, event | category | flops | bytes accessed | tf_op | source)
XLA Modules:
  0.0 85.5 jit_solution(10113931269280355078)
XLA Ops:
  0.0 0.0 copy-start.4
  0.0 1.9 %shard_map.118 = (s32[64,1,128]{2,1,0:T(1,128)S(1)}, f32[64,128]{1,0:T(8,128)S(1)}) custom-call(s32[32,128]{1,0:T(8,128)} %bitcast.13, s32[32,128]{1,0:T(8,128)} %bitcast.14, s32[2,128]{1,0:T(2,128)} %bitcast.15), custom_call_target="tpu_custom_call" | custom-call | flops 1073741824 | bytes 1048576 | tf_op jit(solution)/shard_map/pallas_call | solution.py:252
  1.9 34.6 %all_to_all.15.asked_ref = s32[64,1,128]{2,1,0:T(1,128)S(1)} all-to-all(s32[64,1,128]{2,1,0:T(1,128)S(1)} %get-tuple-element.7), channel_id=1, replica_groups=mesh['rows'=64,'feat'=16] {'rows'}, dimensions={0} | all-to-all | bytes 65536 | tf_op jit(solution)/shard_map/all_to_all | solution.py:347
  36.5 0.0 copy-done.4
  36.5 4.7 %shard_map.119 = bf16[64,32,128]{2,1,0:T(8,128)(2,1)S(1)} custom-call(s32[64,1,128]{2,1,0:T(1,128)S(1)} %all_to_all.15.asked_ref, bf16[48,4096]{1,0:T(8,128)(2,1)S(1)} %bitcast.9), custom_call_target="tpu_custom_call" | custom-call | flops 5368709120 | bytes 1048576 | tf_op jit(solution)/shard_map/pallas_call | solution.py:252
  41.2 19.2 %all_to_all.16.reply_ref = bf16[64,32,128]{2,1,0:T(8,128)(2,1)S(1)} all-to-all(bf16[64,32,128]{2,1,0:T(8,128)(2,1)S(1)} %shard_map.119), channel_id=1, replica_groups=mesh['rows'=64,'feat'=16] {'rows'}, dimensions={0} | all-to-all | bytes 1048576 | tf_op jit(solution)/shard_map/all_to_all | solution.py:349
  60.4 0.0 copy-start
  60.4 0.0 copy-start.1
  60.4 0.0 copy-start.2
  60.4 0.0 copy-start.3
  60.4 0.0 copy-start.5
  60.4 0.0 copy-start.6
  60.4 0.0 copy-start.7
  60.5 0.0 copy-start.8
  60.5 3.7 %shard_map.120 = bf16[256,128]{1,0:T(8,128)(2,1)S(1)} custom-call(bf16[64,32,128]{2,1,0:T(8,128)(2,1)S(1)} %all_to_all.16.reply_ref, f32[64,128]{1,0:T(8,128)S(1)} %get-tuple-element.8.code_ref), custom_call_target="tpu_custom_call" | custom-call | flops 4294967296 | bytes 1048576 | tf_op jit(solution)/shard_map/pallas_call | solution.py:252
  64.2 19.4 %all_to_all.17.part_ref = bf16[16,16,128]{2,1,0:T(8,128)(2,1)S(1)} all-to-all(bf16[16,16,128]{2,1,0:T(8,128)(2,1)S(1)} %bitcast.8), channel_id=1, replica_groups=mesh['rows'=64,'feat'=16] {'feat'}, dimensions={0} | all-to-all | bytes 131072 | tf_op jit(solution)/shard_map/all_to_all | solution.py:352
  83.6 0.0 copy-done
  83.6 0.0 copy-done.1
  83.6 0.0 copy-done.2
  83.6 0.0 copy-done.3
  83.6 0.0 copy-done.5
  83.6 0.0 copy-done.6
  83.6 0.0 copy-done.7
  83.6 0.0 copy-done.8
  83.6 1.9 %shard_map.121 = bf16[16,1024]{1,0:T(8,128)(2,1)} custom-call(bf16[16,16,128]{2,1,0:T(8,128)(2,1)S(1)} %all_to_all.17.part_ref, bf16[768,1024]{1,0:T(8,128)(2,1)S(1)} %copy-done.2, bf16[768,1024]{1,0:T(8,128)(2,1)S(1)} %copy-done.3, f32[1,1024]{1,0:T(1,128)S(1)} %bitcast.10, bf16[1024,1024]{1,0:T(8,128)(2,1)S(1)} %copy-done, ...), custom_call_target="tpu_custom_call" | custom-call | flops 3221225472 | bytes 1048576 | tf_op jit(solution)/shard_map/pallas_call | solution.py:252
Async XLA Ops:
  0.0 36.5 %copy-start.4 = (bf16[4096,48]{0,1:T(8,128)(2,1)S(1)}, bf16[4096,48]{0,1:T(8,128)(2,1)}, u32[]{:S(2)}) copy-start(bf16[4096,48]{0,1:T(8,128)(2,1)} %param.12) | copy-start | bytes 1179652
  60.4 23.1 %copy-start = (bf16[1024,1024]{1,0:T(8,128)(2,1)S(1)}, bf16[1024,1024]{1,0:T(8,128)(2,1)}, u32[]{:S(2)}) copy-start(bf16[1024,1024]{1,0:T(8,128)(2,1)} %w2_self_ref.1) | copy-start | bytes 6291460
  60.4 23.1 %copy-start.1 = (bf16[1024,1024]{1,0:T(8,128)(2,1)S(1)}, bf16[1024,1024]{1,0:T(8,128)(2,1)}, u32[]{:S(2)}) copy-start(bf16[1024,1024]{1,0:T(8,128)(2,1)} %w2_neigh_ref.1) | copy-start | bytes 6291460
  60.4 23.1 %copy-start.2 = (bf16[768,1024]{1,0:T(8,128)(2,1)S(1)}, bf16[768,1024]{1,0:T(8,128)(2,1)}, u32[]{:S(2)}) copy-start(bf16[768,1024]{1,0:T(8,128)(2,1)} %w1_self_ref.1) | copy-start | bytes 4718596
  60.4 23.1 %copy-start.3 = (bf16[768,1024]{1,0:T(8,128)(2,1)S(1)}, bf16[768,1024]{1,0:T(8,128)(2,1)}, u32[]{:S(2)}) copy-start(bf16[768,1024]{1,0:T(8,128)(2,1)} %w1_neigh_ref.1) | copy-start | bytes 4718596
  60.4 23.1 %copy-start.5 = (s32[16,10]{1,0:T(8,128)S(1)}, s32[16,10]{1,0:T(8,128)}, u32[]{:S(2)}) copy-start(s32[16,10]{1,0:T(8,128)} %neighbours_ref.1) | copy-start | bytes 1924
  60.4 23.1 %copy-start.6 = (f32[1024]{0:T(1024)S(1)}, f32[1024]{0:T(1024)}, u32[]{:S(2)}) copy-start(f32[1024]{0:T(1024)} %param.15) | copy-start | bytes 12292
  60.4 23.1 %copy-start.7 = (f32[1024]{0:T(1024)S(1)}, f32[1024]{0:T(1024)}, u32[]{:S(2)}) copy-start(f32[1024]{0:T(1024)} %param.18) | copy-start | bytes 12292
  60.5 23.1 %copy-start.8 = (s32[16]{0:T(128)S(1)}, s32[16]{0:T(128)}, u32[]{:S(2)}) copy-start(s32[16]{0:T(128)} %param.23) | copy-start | bytes 196

commit v3 on v2

--- a/solution.py
+++ b/solution.py
@@ -15,8 +15,9 @@
 WIDTH = 48
 PART = WIDTH // GROUPS
 TRIPLES = -(-PEERS // GROUPS)
-HIGH = 256
-LOWS = 16
+HIGH = 512
+PLANE = 256
+LOWS = 8
 BLOCK = 16
 VMEM = pltpu.VMEM
 LIMIT = 12 * 1024 * 1024
@@ -144,69 +145,66 @@
     spread_halves(asked_ref[:, 0, :], scratch)
     for low in range(LOWS):
         table[low * WIDTH : (low + 1) * WIDTH, :] = features_ref[:, low * HIGH : (low + 1) * HIGH]
+    one = jnp.bfloat16(1.0)
+    zero = jnp.bfloat16(0.0)
+    number = iota((PLANE, 2 * LANES), 0).astype(jnp.float32).astype(jnp.bfloat16)
 
     def step(triple, last):
         index = jnp.concatenate([triple_row(scratch, h, triple) for h in range(2)], axis=1)
-        chosen = jnp.where(iota((HIGH, 2 * LANES), 0) == (index & (HIGH - 1)), 1.0, 0.0)
-        rows = jnp.dot(table[...], chosen.astype(jnp.bfloat16), preferred_element_type=jnp.float32)
-        low = index >> 8
-        out = jnp.zeros((WIDTH, 2 * LANES), jnp.float32)
-        for k in range(LOWS):
+        chosen = []
+        for k in range(HIGH // PLANE):
+            here = (index >> 8) & (HIGH // PLANE - 1)
+            key = jnp.where(here == k, index & (PLANE - 1), -1).astype(jnp.float32).astype(jnp.bfloat16)
+            chosen.append(jnp.where(number == key, one, zero))
+        chosen = jnp.concatenate(chosen, axis=0) if len(chosen) > 1 else chosen[0]
+        rows = jnp.dot(table[...], chosen, preferred_element_type=jnp.float32)
+        low = index // HIGH
+        out = rows[:WIDTH]
+        for k in range(1, LOWS):
             out = jnp.where(low == k, rows[k * WIDTH : (k + 1) * WIDTH], out)
+        out = out.astype(jnp.bfloat16)
         for h in range(2):
             half = out[:, h * LANES : (h + 1) * LANES]
             tiles = swap_groups([half[b * PART : (b + 1) * PART] for b in range(GROUPS)])
             for x in range(1 if last else GROUPS):
-                found_ref[GROUPS * triple + x, h * PART : (h + 1) * PART, :] = tiles[x].astype(
-                    jnp.bfloat16
-                )
-
-    def body(i, carry):
-        for k in range(3):
-            step(3 * i + k, False)
-        return carry
-
-    lax.fori_loop(0, (TRIPLES - 1) // 3, body, 0)
-    step(TRIPLES - 1, True)
-
-
-def mean_kernel(reply_ref, code_ref, out_ref, scratch, total):
+                found_ref[GROUPS * triple + x, h * PART : (h + 1) * PART, :] = tiles[x]
+
+    for triple in range(TRIPLES):
+        step(triple, triple == TRIPLES - 1)
+
+
+def mean_kernel(reply_ref, code_ref, out_ref, scratch):
     spread_halves(code_ref[...], scratch)
     targets = out_ref.shape[0]
-    total[...] = jnp.zeros_like(total)
+    row = iota((2 * targets, 2 * LANES), 0)
+    wanted = jnp.where(row < targets, -(row + 1), row - targets + 1)
+    wanted = wanted.astype(jnp.float32).astype(jnp.bfloat16)
+    one = jnp.bfloat16(1.0)
+    zero = jnp.bfloat16(0.0)
 
     def step(triple, last):
         code = jnp.concatenate([triple_row(scratch, h, triple) for h in range(2)], axis=1)
-        row = iota((2 * targets, 2 * LANES), 0)
-        wanted = jnp.where(row < targets, -(row + 1), row - targets + 1).astype(jnp.float32)
-        member = jnp.where(wanted == code, 1.0, 0.0).astype(jnp.bfloat16)
+        member = jnp.where(wanted == code.astype(jnp.bfloat16), one, zero)
         halves = []
         for h in range(2):
             tiles = [
-                reply_ref[
-                    GROUPS * triple + (0 if last else x), h * PART : (h + 1) * PART, :
-                ].astype(jnp.float32)
+                reply_ref[GROUPS * triple + (0 if last else x), h * PART : (h + 1) * PART, :]
                 for x in range(GROUPS)
             ]
             columns = swap_groups(tiles)
             halves.append(
-                jnp.concatenate(
-                    columns + columns + [jnp.ones((2 * PART, LANES), jnp.float32)], axis=0
-                ).astype(jnp.bfloat16)
+                jnp.concatenate(columns + columns + [jnp.ones((2 * PART, LANES), jnp.bfloat16)], axis=0)
             )
-        total[...] += lax.dot_general(
-            member, jnp.concatenate(halves, axis=1), NT, preferred_element_type=jnp.float32
-        )
-
-    def body(i, carry):
-        for k in range(3):
-            step(3 * i + k, False)
-        return carry
-
-    lax.fori_loop(0, (TRIPLES - 1) // 3, body, 0)
-    step(TRIPLES - 1, True)
-    own = total[:targets]
-    neigh = total[targets:]
+        return member, jnp.concatenate(halves, axis=1)
+
+    def add(parts):
+        members = jnp.concatenate([p[0] for p in parts], axis=1)
+        columns = jnp.concatenate([p[1] for p in parts], axis=1)
+        return lax.dot_general(members, columns, NT, preferred_element_type=jnp.float32)
+
+    sums = add([step(i, i == TRIPLES - 1) for i in range(TRIPLES)])
+    own = sums[:targets]
+    neigh = sums[targets:]
     mean = neigh / neigh[:, 2 * WIDTH : 2 * WIDTH + 1]
     out_ref[...] = jnp.where(iota(own.shape, 1) < WIDTH, own, mean).astype(jnp.bfloat16)
 
@@ -303,7 +301,6 @@
         jax.ShapeDtypeStruct((targets, LANES), jnp.bfloat16),
         [
             pltpu.VMEM((2, PEERS + 8, LANES), jnp.float32),
-            pltpu.VMEM((2 * targets, LANES), jnp.float32),
         ],
         4 << 30,
         replies,

time: 85.7 us -> 81.9 us (0.956)
  Pallas kernels: 12.1 us -> 8.2 us
    pallas_call x4, Pallas kernels: 12.1 us -> 8.2 us  [call(): pl.pallas_call(kernel, out_shape=out_shape, in_specs=[pl.BlockSpec(memory...]
where the time goes in v3:
time: 81.9 us; the launch traced here: 81.7 us
  blocking collectives  73.4 us (90%)
  Pallas kernels  8.2 us (10%)
    all_to_all x1, blocking collectives, per_device(): lax.all_to_all(requests, 'rows', split_axis=0, concat_axis=0, tiled=True)  34.6 us
    all_to_all x1, blocking collectives, per_device(): lax.all_to_all(mine, 'feat', split_axis=0, concat_axis=0, tiled=True)  19.5 us
    all_to_all x1, blocking collectives, per_device(): lax.all_to_all(found, 'rows', split_axis=0, concat_axis=0, tiled=True)  19.2 us
    pallas_call x4, Pallas kernels, call(): pl.pallas_call(kernel, out_shape=out_shape, in_specs=[pl.BlockSpec(memory...  8.2 us

profile of v3, /device:TPU:1, one launch (start us, length us, event | category | flops | bytes accessed | tf_op | source)
XLA Modules:
  0.0 81.7 jit_solution(3867868982570318877)
XLA Ops:
  0.0 0.0 copy-start.4
  0.0 1.9 %shard_map.118 = (s32[64,1,128]{2,1,0:T(1,128)S(1)}, f32[64,128]{1,0:T(8,128)S(1)}) custom-call(s32[32,128]{1,0:T(8,128)} %bitcast.13, s32[32,128]{1,0:T(8,128)} %bitcast.14, s32[2,128]{1,0:T(2,128)} %bitcast.15), custom_call_target="tpu_custom_call" | custom-call | flops 1073741824 | bytes 1048576 | tf_op jit(solution)/shard_map/pallas_call | solution.py:250
  1.9 34.6 %all_to_all.15.asked_ref = s32[64,1,128]{2,1,0:T(1,128)S(1)} all-to-all(s32[64,1,128]{2,1,0:T(1,128)S(1)} %get-tuple-element.7), channel_id=1, replica_groups=mesh['rows'=64,'feat'=16] {'rows'}, dimensions={0} | all-to-all | bytes 65536 | tf_op jit(solution)/shard_map/all_to_all | solution.py:344
  36.5 0.0 copy-done.4
  36.5 2.6 %shard_map.119 = bf16[64,32,128]{2,1,0:T(8,128)(2,1)S(1)} custom-call(s32[64,1,128]{2,1,0:T(1,128)S(1)} %all_to_all.15.asked_ref, bf16[48,4096]{1,0:T(8,128)(2,1)S(1)} %bitcast.9), custom_call_target="tpu_custom_call" | custom-call | flops 5368709120 | bytes 1048576 | tf_op jit(solution)/shard_map/pallas_call | solution.py:250
  39.1 19.2 %all_to_all.16.reply_ref = bf16[64,32,128]{2,1,0:T(8,128)(2,1)S(1)} all-to-all(bf16[64,32,128]{2,1,0:T(8,128)(2,1)S(1)} %shard_map.119), channel_id=1, replica_groups=mesh['rows'=64,'feat'=16] {'rows'}, dimensions={0} | all-to-all | bytes 1048576 | tf_op jit(solution)/shard_map/all_to_all | solution.py:346
  58.4 0.0 copy-start
  58.4 0.0 copy-start.1
  58.4 0.0 copy-start.2
  58.4 0.0 copy-start.3
  58.4 0.0 copy-start.5
  58.4 0.0 copy-start.6
  58.4 0.0 copy-start.7
  58.4 0.0 copy-start.8
  58.4 1.8 %shard_map.120 = bf16[256,128]{1,0:T(8,128)(2,1)S(1)} custom-call(bf16[64,32,128]{2,1,0:T(8,128)(2,1)S(1)} %all_to_all.16.reply_ref, f32[64,128]{1,0:T(8,128)S(1)} %get-tuple-element.8.code_ref), custom_call_target="tpu_custom_call" | custom-call | flops 4294967296 | bytes 1048576 | tf_op jit(solution)/shard_map/pallas_call | solution.py:250
  60.3 19.5 %all_to_all.17.part_ref = bf16[16,16,128]{2,1,0:T(8,128)(2,1)S(1)} all-to-all(bf16[16,16,128]{2,1,0:T(8,128)(2,1)S(1)} %bitcast.8), channel_id=1, replica_groups=mesh['rows'=64,'feat'=16] {'feat'}, dimensions={0} | all-to-all | bytes 131072 | tf_op jit(solution)/shard_map/all_to_all | solution.py:349
  79.8 0.0 copy-done
  79.8 0.0 copy-done.1
  79.8 0.0 copy-done.2
  79.8 0.0 copy-done.3
  79.8 0.0 copy-done.5
  79.8 0.0 copy-done.6
  79.8 0.0 copy-done.7
  79.8 0.0 copy-done.8
  79.8 1.9 %shard_map.121 = bf16[16,1024]{1,0:T(8,128)(2,1)} custom-call(bf16[16,16,128]{2,1,0:T(8,128)(2,1)S(1)} %all_to_all.17.part_ref, bf16[768,1024]{1,0:T(8,128)(2,1)S(1)} %copy-done.2, bf16[768,1024]{1,0:T(8,128)(2,1)S(1)} %copy-done.3, f32[1,1024]{1,0:T(1,128)S(1)} %bitcast.10, bf16[1024,1024]{1,0:T(8,128)(2,1)S(1)} %copy-done, ...), custom_call_target="tpu_custom_call" | custom-call | flops 3221225472 | bytes 1048576 | tf_op jit(solution)/shard_map/pallas_call | solution.py:250
Async XLA Ops:
  0.0 36.5 %copy-start.4 = (bf16[4096,48]{0,1:T(8,128)(2,1)S(1)}, bf16[4096,48]{0,1:T(8,128)(2,1)}, u32[]{:S(2)}) copy-start(bf16[4096,48]{0,1:T(8,128)(2,1)} %param.12) | copy-start | bytes 1179652
  58.4 21.4 %copy-start = (bf16[1024,1024]{1,0:T(8,128)(2,1)S(1)}, bf16[1024,1024]{1,0:T(8,128)(2,1)}, u32[]{:S(2)}) copy-start(bf16[1024,1024]{1,0:T(8,128)(2,1)} %w2_self_ref.1) | copy-start | bytes 6291460
  58.4 21.4 %copy-start.1 = (bf16[1024,1024]{1,0:T(8,128)(2,1)S(1)}, bf16[1024,1024]{1,0:T(8,128)(2,1)}, u32[]{:S(2)}) copy-start(bf16[1024,1024]{1,0:T(8,128)(2,1)} %w2_neigh_ref.1) | copy-start | bytes 6291460
  58.4 21.4 %copy-start.2 = (bf16[768,1024]{1,0:T(8,128)(2,1)S(1)}, bf16[768,1024]{1,0:T(8,128)(2,1)}, u32[]{:S(2)}) copy-start(bf16[768,1024]{1,0:T(8,128)(2,1)} %w1_self_ref.1) | copy-start | bytes 4718596
  58.4 21.4 %copy-start.3 = (bf16[768,1024]{1,0:T(8,128)(2,1)S(1)}, bf16[768,1024]{1,0:T(8,128)(2,1)}, u32[]{:S(2)}) copy-start(bf16[768,1024]{1,0:T(8,128)(2,1)} %w1_neigh_ref.1) | copy-start | bytes 4718596
  58.4 21.4 %copy-start.5 = (s32[16,10]{1,0:T(8,128)S(1)}, s32[16,10]{1,0:T(8,128)}, u32[]{:S(2)}) copy-start(s32[16,10]{1,0:T(8,128)} %neighbours_ref.1) | copy-start | bytes 1924
  58.4 21.4 %copy-start.6 = (f32[1024]{0:T(1024)S(1)}, f32[1024]{0:T(1024)}, u32[]{:S(2)}) copy-start(f32[1024]{0:T(1024)} %param.15) | copy-start | bytes 12292
  58.4 21.4 %copy-start.7 = (f32[1024]{0:T(1024)S(1)}, f32[1024]{0:T(1024)}, u32[]{:S(2)}) copy-start(f32[1024]{0:T(1024)} %param.18) | copy-start | bytes 12292
  58.4 21.4 %copy-start.8 = (s32[16]{0:T(128)S(1)}, s32[16]{0:T(128)}, u32[]{:S(2)}) copy-start(s32[16]{0:T(128)} %param.23) | copy-start | bytes 196

commit v4 on v3

v4 whole, which is shorter than its diff:
```python
import jax
import jax.numpy as jnp
from jax import lax
from jax.experimental import pallas as pl
from jax.experimental.pallas import tpu as pltpu
from jax.sharding import PartitionSpec as P

K1 = 15
K2 = 10
LANES = 128
PEERS = 64
CAPACITY = 80
USUAL = 64
FLAG = LANES - 1
WIDTH = 48
PART = WIDTH // 2
HIGH = 512
PLANE = 256
LOWS = 8
BLOCK = 16
VMEM = pltpu.VMEM
LIMIT = 12 * 1024 * 1024
NT = (((1,), (1,)), ((), ()))


def iota(shape, dimension):
    return lax.broadcasted_iota(jnp.int32, shape, dimension)


def route_kernel(
    owner_hbm, row_hbm, count_hbm, request_ref, code_ref, owner_ref, row_ref, count_ref, arrived
):
    copies = [
        pltpu.make_async_copy(source, target, arrived.at[i])
        for i, (source, target) in enumerate(
            ((owner_hbm, owner_ref), (row_hbm, row_ref), (count_hbm, count_ref))
        )
    ]
    for copy in copies:
        copy.start()
    for copy in copies:
        copy.wait()
    chunks = owner_ref.shape[0]
    per_chunk = LANES // (K1 + 1)
    half = chunks // 2
    chunk = iota((chunks, LANES), 0)
    lane = iota((chunks, LANES), 1)
    count = count_ref[...].astype(jnp.float32)
    spread = jnp.concatenate(
        [jnp.broadcast_to(count[i : i + 1], (half, LANES)) for i in range(2)], axis=0
    )
    spread = jnp.where(lane // per_chunk == chunk % half, spread, 0.0)
    pick = jnp.where(
        iota((LANES, LANES), 0) % per_chunk == iota((LANES, LANES), 1) // (K1 + 1), 1.0, 0.0
    )
    limit = jnp.dot(
        spread.astype(jnp.bfloat16), pick.astype(jnp.bfloat16), preferred_element_type=jnp.float32
    )
    place = lane % (K1 + 1)
    target = (chunk * per_chunk + lane // (K1 + 1) + 1).astype(jnp.float32)
    code = jnp.where(
        place == 0, -target, jnp.where(place.astype(jnp.float32) <= limit, target, 0.0)
    )
    owner = jnp.where(code == 0.0, -1, owner_ref[...])
    mask = owner[:, None, :] == iota((chunks, PEERS, LANES), 1)
    ones = jnp.where(mask, 1.0, 0.0)
    before = iota((LANES, 2 * LANES), 0)
    upto = iota((LANES, 2 * LANES), 1)
    prefix = jnp.where((before < upto) | (upto >= LANES), 1.0, 0.0).astype(jnp.bfloat16)
    sums = jnp.dot(
        ones.astype(jnp.bfloat16).reshape(chunks * PEERS, LANES),
        prefix,
        preferred_element_type=jnp.float32,
    ).reshape(chunks, PEERS, 2 * LANES)

    row = row_ref[...]
    high = (row >> 6).astype(jnp.float32)
    low = (row & 63).astype(jnp.float32)

    offset = jnp.zeros((PEERS, LANES), jnp.float32)
    total = jnp.zeros((3 * PEERS, CAPACITY), jnp.float32)
    slot = iota((CAPACITY, LANES), 0).astype(jnp.float32)
    values, slots = [], []
    for c in range(chunks):
        here = mask[c]
        rank = jnp.sum(
            jnp.where(here, sums[c, :, :LANES] + offset, 0.0), axis=0, keepdims=True
        )
        offset = offset + sums[c, :, LANES:]
        slots.append(jnp.where(slot == rank, 1.0, 0.0).astype(jnp.bfloat16))
        values.append(
            jnp.concatenate(
                [jnp.where(here, v[c : c + 1], 0.0) for v in (high, low, code)], axis=0
            ).astype(jnp.bfloat16)
        )
        if c % 2 == 1:
            total = total + lax.dot_general(
                jnp.concatenate(values, axis=1),
                jnp.concatenate(slots, axis=1),
                NT,
                preferred_element_type=jnp.float32,
            )
            values, slots = [], []
    crowded = jnp.where(jnp.max(offset) > USUAL, 1, 0)
    request_ref[...] = jnp.where(iota(request_ref.shape, 2) == FLAG, crowded, 0)
    code_ref[...] = jnp.zeros_like(code_ref)
    request_ref[:, 0, :CAPACITY] = (
        total[:PEERS] * 64.0 + total[PEERS : 2 * PEERS]
    ).astype(jnp.int32)
    code_ref[:, :CAPACITY] = total[2 * PEERS :]


def spread(slots, scratch):
    lane = iota(slots.shape, 1)
    scratch[...] = jnp.where(lane < USUAL, slots, pltpu.roll(slots, USUAL, 1))


def two_peers(scratch, peer):
    lane = iota((1, LANES), 1)
    return jnp.where(lane < USUAL, scratch[peer : peer + 1, :], scratch[peer + 1 : peer + 2, :])


def swap(first, second):
    lane = iota(first.shape, 1)
    return (
        jnp.where(lane < USUAL, first, pltpu.roll(second, USUAL, 1)),
        jnp.where(lane < USUAL, pltpu.roll(first, USUAL, 1), second),
    )


def find_kernel(asked_ref, features_ref, found_ref, crowded_ref, table, scratch):
    asked = asked_ref[:, 0, :]
    crowded_ref[0, 0] = jnp.max(jnp.where(iota(asked.shape, 1) == FLAG, asked, 0))
    spread(asked, scratch)
    for low in range(LOWS):
        table[low * WIDTH : (low + 1) * WIDTH, :] = features_ref[:, low * HIGH : (low + 1) * HIGH]
    one = jnp.bfloat16(1.0)
    zero = jnp.bfloat16(0.0)
    number = iota((PLANE, 2 * LANES), 0).astype(jnp.float32).astype(jnp.bfloat16)
    for peer in range(0, PEERS, 4):
        index = jnp.concatenate([two_peers(scratch, peer + 2 * h) for h in range(2)], axis=1)
        chosen = []
        for k in range(HIGH // PLANE):
            here = (index >> 8) & (HIGH // PLANE - 1)
            key = jnp.where(here == k, index & (PLANE - 1), -1).astype(jnp.float32).astype(jnp.bfloat16)
            chosen.append(jnp.where(number == key, one, zero))
        rows = jnp.dot(
            table[...], jnp.concatenate(chosen, axis=0), preferred_element_type=jnp.float32
        )
        low = index // HIGH
        out = rows[:WIDTH]
        for k in range(1, LOWS):
            out = jnp.where(low == k, rows[k * WIDTH : (k + 1) * WIDTH], out)
        for h in range(2):
            half = out[:, h * LANES : (h + 1) * LANES]
            for x, tile in enumerate(swap(half[:PART], half[PART:])):
                found_ref[peer + 2 * h + x, :, :] = tile.astype(jnp.bfloat16)


def sums_of(reply_ref, code_ref, scratch, targets):
    spread(code_ref[...], scratch)
    row = iota((2 * targets, 2 * LANES), 0)
    wanted = jnp.where(row < targets, -(row + 1), row - targets + 1)
    wanted = wanted.astype(jnp.float32).astype(jnp.bfloat16)
    one = jnp.bfloat16(1.0)
    zero = jnp.bfloat16(0.0)
    members, columns = [], []
    for peer in range(0, PEERS, 4):
        code = jnp.concatenate([two_peers(scratch, peer + 2 * h) for h in range(2)], axis=1)
        members.append(jnp.where(wanted == code.astype(jnp.bfloat16), one, zero))
        for h in range(2):
            tiles = [reply_ref[peer + 2 * h + x].astype(jnp.float32) for x in range(2)]
            rows = [tile.astype(jnp.bfloat16) for tile in [jnp.concatenate(swap(*tiles), axis=0)]]
            columns.append(
                jnp.concatenate(rows + rows + [jnp.ones((32, LANES), jnp.bfloat16)], axis=0)
            )
    return lax.dot_general(
        jnp.concatenate(members, axis=1),
        jnp.concatenate(columns, axis=1),
        NT,
        preferred_element_type=jnp.float32,
    )


def finish(sums, targets):
    own = sums[:targets]
    neigh = sums[targets:]
    mean = neigh / neigh[:, 2 * WIDTH : 2 * WIDTH + 1]
    return jnp.where(iota(own.shape, 1) < WIDTH, own, mean).astype(jnp.bfloat16)


def mean_kernel(reply_ref, code_ref, out_ref, sums_ref, scratch):
    sums = sums_of(reply_ref, code_ref, scratch, out_ref.shape[0])
    sums_ref[...] = sums
    out_ref[...] = finish(sums, out_ref.shape[0])


def rest_kernel(reply_ref, code_ref, sums_ref, out_ref, scratch):
    sums = sums_ref[...] + sums_of(reply_ref, code_ref, scratch, out_ref.shape[0])
    out_ref[...] = finish(sums, out_ref.shape[0])


def layers_kernel(
    part_ref,
    w1_self_ref,
    w1_neigh_ref,
    bias_one_ref,
    w2_self_ref,
    w2_neigh_ref,
    bias_two_ref,
    neighbours_ref,
    count_ref,
    out_ref,
):
    parts = [part_ref[i].astype(jnp.float32) for i in range(part_ref.shape[0])]
    own = jnp.concatenate([p[:, :WIDTH] for p in parts], axis=1).astype(jnp.bfloat16)
    mean = jnp.concatenate([p[:, WIDTH : 2 * WIDTH] for p in parts], axis=1).astype(jnp.bfloat16)
    pre = jnp.dot(own, w1_self_ref[...], preferred_element_type=jnp.float32) + jnp.dot(
        mean, w1_neigh_ref[...], preferred_element_type=jnp.float32
    )
    hidden = jnp.maximum(pre + bias_one_ref[...], 0.0).astype(jnp.bfloat16)
    lane = iota((BLOCK, BLOCK), 1)
    count = jnp.sum(
        jnp.where(lane == iota((BLOCK, BLOCK), 0), count_ref[...].astype(jnp.float32), 0.0),
        axis=1,
        keepdims=True,
    )
    member = jnp.zeros((BLOCK, BLOCK), jnp.float32)
    for j in range(K2):
        named = (neighbours_ref[:, j : j + 1] == lane) & (count > j)
        member = member + jnp.where(named, 1.0, 0.0)
    sums = jnp.dot(member.astype(jnp.bfloat16), hidden, preferred_element_type=jnp.float32)
    mean_two = (sums / count).astype(jnp.bfloat16)
    total = jnp.dot(hidden, w2_self_ref[...], preferred_element_type=jnp.float32) + jnp.dot(
        mean_two, w2_neigh_ref[...], preferred_element_type=jnp.float32
    )
    out_ref[...] = (total + bias_two_ref[...]).astype(jnp.bfloat16)


def call(kernel, out_shape, scratch_shapes, flops, *operands, space=VMEM, out_specs=None):
    return pl.pallas_call(
        kernel,
        out_shape=out_shape,
        in_specs=[pl.BlockSpec(memory_space=space)] * len(operands),
        out_specs=out_specs or jax.tree.map(lambda _: pl.BlockSpec(memory_space=VMEM), out_shape),
        scratch_shapes=scratch_shapes,
        compiler_params=pltpu.CompilerParams(vmem_limit_bytes=LIMIT),
        cost_estimate=pl.CostEstimate(flops=flops, bytes_accessed=1 << 20, transcendentals=0),
    )(*operands)


def route(owner, row_index, count_one):
    lines = owner.shape[0] // LANES
    return call(
        route_kernel,
        [
            jax.ShapeDtypeStruct((PEERS, 1, LANES), jnp.int32),
            jax.ShapeDtypeStruct((PEERS, LANES), jnp.float32),
        ],
        [
            pltpu.VMEM((lines, LANES), jnp.int32),
            pltpu.VMEM((lines, LANES), jnp.int32),
            pltpu.VMEM((count_one.shape[0] // LANES, LANES), jnp.int32),
            pltpu.SemaphoreType.DMA((3,)),
        ],
        1 << 30,
        *[
            pltpu.with_memory_space_constraint(a.reshape(-1, LANES), pltpu.HBM)
            for a in (owner, row_index, count_one)
        ],
        space=pltpu.HBM,
    )


def find(asked, features):
    return call(
        find_kernel,
        [
            jax.ShapeDtypeStruct((PEERS, PART, LANES), jnp.bfloat16),
            jax.ShapeDtypeStruct((1, 1), jnp.int32),
        ],
        [
            pltpu.VMEM((LOWS * WIDTH, HIGH), jnp.bfloat16),
            pltpu.VMEM((PEERS, LANES), jnp.int32),
        ],
        5 << 30,
        asked,
        features.T,
        out_specs=[pl.BlockSpec(memory_space=VMEM), pl.BlockSpec(memory_space=pltpu.SMEM)],
    )


def means(replies, code, targets):
    return call(
        mean_kernel,
        [
            jax.ShapeDtypeStruct((targets, LANES), jnp.bfloat16),
            jax.ShapeDtypeStruct((2 * targets, LANES), jnp.float32),
        ],
        [pltpu.VMEM((PEERS, LANES), jnp.float32)],
        4 << 30,
        replies,
        code,
    )


def with_rest(replies, code, sums, targets):
    return call(
        rest_kernel,
        jax.ShapeDtypeStruct((targets, LANES), jnp.bfloat16),
        [pltpu.VMEM((PEERS, LANES), jnp.float32)],
        4 << 30,
        replies,
        code,
        sums,
    )


def layers(parts, w1_self, w1_neigh, bias_one, w2_self, w2_neigh, bias_two, neighbours, count):
    return call(
        layers_kernel,
        jax.ShapeDtypeStruct((BLOCK, w2_self.shape[1]), jnp.bfloat16),
        [],
        3 << 30,
        parts,
        w1_self,
        w1_neigh,
        bias_one.reshape(1, -1),
        w2_self,
        w2_neigh,
        bias_two.reshape(1, -1),
        neighbours,
        count.reshape(1, -1),
    )


def later_slots(slots):
    lane = lax.broadcasted_iota(jnp.int32, slots.shape, slots.ndim - 1)
    return jnp.where(
        lane < CAPACITY - USUAL, jnp.roll(slots, -USUAL, axis=-1), jnp.zeros_like(slots)
    )


def exchange(array, axis):
    return lax.all_to_all(array, axis, split_axis=0, concat_axis=0, tiled=True)


def per_device(
    features,
    w1_self,
    w1_neigh,
    bias_one,
    w2_self,
    w2_neigh,
    bias_two,
    owner,
    row_index,
    count_one,
    neighbours_two,
    count_two,
):
    targets = count_one.shape[0]
    requests, code = route(owner, row_index, count_one)
    asked = exchange(requests, "rows")
    found, crowded = find(asked, features)
    mine, sums = means(exchange(found, "rows"), code, targets)

    def more(asked, features, code, sums, mine):
        found, _ = find(later_slots(asked), features)
        return with_rest(exchange(found, "rows"), later_slots(code), sums, targets)

    def no_more(asked, features, code, sums, mine):
        return mine

    mine = lax.cond(crowded[0, 0] > 0, more, no_more, asked, features, code, sums, mine)
    parts = exchange(mine.reshape(-1, BLOCK, LANES), "feat")
    return layers(
        parts, w1_self, w1_neigh, bias_one, w2_self, w2_neigh, bias_two, neighbours_two, count_two
    )


def solution(mesh):
    return jax.shard_map(
        per_device,
        mesh=mesh,
        in_specs=(
            P("rows", "feat"),
            P(),
            P(),
            P(),
            P(),
            P(),
            P(),
            P("rows", None),
            P("rows"),
            P("rows"),
            P(("rows", "feat"), None),
            P(("rows", "feat")),
        ),
        out_specs=P(("rows", "feat"), None),
        check_vma=False,
    )
```

time: 81.9 us -> 84.9 us (1.037)
  blocking collectives: 73.4 us -> 53.7 us
  waiting for transfers between devices: 0 us -> 13 us
  starting transfers between devices: 0 us -> 4.64 us
  local copies, waits for them, and re-layouts: 0.04 us -> 4.44 us
    all_to_all x3 -> x2, blocking collectives: 73.4 us -> 53.7 us  [exchange(): return lax.all_to_all(array, axis, split_axis=0, concat_axis=0, tiled=True)]
    all_to_all x0 -> x1, waiting for transfers between devices: none -> 13 us  [exchange(): return lax.all_to_all(array, axis, split_axis=0, concat_axis=0, tiled=True)]
    all_to_all x0 -> x1, starting transfers between devices: none -> 4.64 us  [exchange(): return lax.all_to_all(array, axis, split_axis=0, concat_axis=0, tiled=True)]
    unnamed x18, local copies, waits for them, and re-layouts: 0.04 us -> 4.44 us
  transfers between devices with their start and end apart: 0 -> 1, of which waited for: 0 -> 1; matrix products, arithmetic and copies ran while one was open for 0% -> 0% of each run, Pallas kernels for 0% -> 0%
where the time goes in v4:
time: 84.9 us; the launch traced here: 84.5 us
  blocking collectives  53.7 us (63%)
  waiting for transfers between devices  13 us (15%)
  Pallas kernels  8.03 us (9%)
  starting transfers between devices  4.64 us (5%)
  local copies, waits for them, and re-layouts  4.44 us (5%)
    all_to_all x2, blocking collectives, exchange(): return lax.all_to_all(array, axis, split_axis=0, concat_axis=0, tiled=True)  53.7 us
    all_to_all x1, waiting for transfers between devices, exchange(): return lax.all_to_all(array, axis, split_axis=0, concat_axis=0, tiled=True)  13 us
    pallas_call x4, Pallas kernels, call(): pl.pallas_call(kernel, out_shape=out_shape, in_specs=[pl.BlockSpec(memory...  8.03 us
    all_to_all x1, starting transfers between devices, exchange(): return lax.all_to_all(array, axis, split_axis=0, concat_axis=0, tiled=True)  4.64 us
    unnamed x18, local copies, waits for them, and re-layouts  4.44 us
  transfers between devices with their start and end apart: 1, of which 1 were waited for; matrix products, arithmetic and copies ran while one was open for 0% of the time, Pallas kernels for 0%

profile of v4, /device:TPU:1, one launch (start us, length us, event | category | flops | bytes accessed | tf_op | source)
XLA Modules:
  0.0 84.5 jit_solution(5809136459402864396)
XLA Ops:
  0.0 0.0 copy-start.8
  0.0 2.0 %shard_map.118 = (s32[64,1,128]{2,1,0:T(1,128)S(1)}, f32[64,128]{1,0:T(8,128)S(1)}) custom-call(s32[32,128]{1,0:T(8,128)} %bitcast.16, s32[32,128]{1,0:T(8,128)} %bitcast.17, s32[2,128]{1,0:T(2,128)} %bitcast.18), custom_call_target="tpu_custom_call" | custom-call | flops 1073741824 | bytes 1048576 | tf_op jit(solution)/shard_map/pallas_call | solution.py:241
  2.0 34.6 %all_to_all.19.asked_ref = s32[64,1,128]{2,1,0:T(1,128)S(1)} all-to-all(s32[64,1,128]{2,1,0:T(1,128)S(1)} %get-tuple-element.28), channel_id=1, replica_groups=mesh['rows'=64,'feat'=16] {'rows'}, dimensions={0} | all-to-all | bytes 65536 | tf_op jit(solution)/shard_map/all_to_all | solution.py:345
  36.6 0.0 copy-done.8
  36.6 2.8 %shard_map.119 = (bf16[64,24,128]{2,1,0:T(8,128)(2,1)}, s32[1,1]{1,0:T(1,128)}) custom-call(s32[64,1,128]{2,1,0:T(1,128)S(1)} %all_to_all.19.asked_ref, bf16[48,4096]{1,0:T(8,128)(2,1)S(1)} %bitcast.14), custom_call_target="tpu_custom_call" | custom-call | flops 5368709120 | bytes 1048576 | tf_op jit(solution)/shard_map/pallas_call | solution.py:241
  39.4 4.6 %all-to-all-start.2 = ((bf16[64,24,128]{2,1,0:T(8,128)(2,1)}), bf16[64,24,128]{2,1,0:T(8,128)(2,1)S(1)}, u32[]{:S(2)}, u32[]{:S(2)}) async-start(bf16[64,24,128]{2,1,0:T(8,128)(2,1)} %get-tuple-element.30), calls=%async_computation.2 | async-start | bytes 786432 | tf_op jit(solution)/shard_map/all_to_all | solution.py:345
  44.7 13.0 %all-to-all-done.2.reply_ref = bf16[64,24,128]{2,1,0:T(8,128)(2,1)S(1)} async-done(((bf16[64,24,128]{2,1,0:T(8,128)(2,1)}), bf16[64,24,128]{2,1,0:T(8,128)(2,1)S(1)}, u32[]{:S(2)}, u32[]{:S(2)}) %all-to-all-start.2) | async-done | bytes 393248 | tf_op jit(solution)/shard_map/all_to_all | solution.py:345
  57.7 1.4 %shard_map.120 = (bf16[256,128]{1,0:T(8,128)(2,1)S(1)}, f32[512,128]{1,0:T(8,128)S(1)}) custom-call(bf16[64,24,128]{2,1,0:T(8,128)(2,1)S(1)} %all-to-all-done.2.reply_ref, f32[64,128]{1,0:T(8,128)S(1)} %get-tuple-element.31.code_ref), custom_call_target="tpu_custom_call" | custom-call | flops 4294967296 | bytes 1048576 | tf_op jit(solution)/shard_map/pallas_call | solution.py:241
  59.1 0.0 copy-start
  59.1 0.0 copy-start.4
  59.1 0.0 copy-start.5
  59.1 0.0 copy-start.6
  59.1 0.0 copy-start.7
  59.1 19.1 %all_to_all.20.part_ref = bf16[16,16,128]{2,1,0:T(8,128)(2,1)S(1)} all-to-all(bf16[16,16,128]{2,1,0:T(8,128)(2,1)S(1)} %bitcast.13), channel_id=1, replica_groups=mesh['rows'=64,'feat'=16] {'feat'}, dimensions={0} | all-to-all | bytes 131072 | tf_op jit(solution)/shard_map/all_to_all | solution.py:345
  78.2 0.0 copy-done
  78.2 0.0 copy-done.4
  78.2 0.0 copy-done.5
  78.2 0.0 copy-done.6
  78.3 0.0 copy-done.7
  78.3 0.0 copy-start.1
  78.3 1.6 %copy-done.1 = bf16[1024,1024]{1,0:T(8,128)(2,1)S(1)} copy-done((bf16[1024,1024]{1,0:T(8,128)(2,1)S(1)}, bf16[1024,1024]{1,0:T(8,128)(2,1)}, u32[]{:S(2)}) %copy-start.1) | copy-done | bytes 2097176
  79.9 0.0 copy-start.2
  79.9 1.4 %copy-done.2 = bf16[768,1024]{1,0:T(8,128)(2,1)S(1)} copy-done((bf16[768,1024]{1,0:T(8,128)(2,1)S(1)}, bf16[768,1024]{1,0:T(8,128)(2,1)}, u32[]{:S(2)}) %copy-start.2) | copy-done | bytes 1572888
  81.3 0.0 copy-start.3
  81.3 1.4 %copy-done.3 = bf16[768,1024]{1,0:T(8,128)(2,1)S(1)} copy-done((bf16[768,1024]{1,0:T(8,128)(2,1)S(1)}, bf16[768,1024]{1,0:T(8,128)(2,1)}, u32[]{:S(2)}) %copy-start.3) | copy-done | bytes 1572888
  82.7 1.9 %shard_map.121 = bf16[16,1024]{1,0:T(8,128)(2,1)} custom-call(bf16[16,16,128]{2,1,0:T(8,128)(2,1)S(1)} %all_to_all.20.part_ref, bf16[768,1024]{1,0:T(8,128)(2,1)S(1)} %copy-done.2, bf16[768,1024]{1,0:T(8,128)(2,1)S(1)} %copy-done.3, f32[1,1024]{1,0:T(1,128)S(1)} %bitcast.10, bf16[1024,1024]{1,0:T(8,128)(2,1)S(1)} %copy-done, ...), custom_call_target="tpu_custom_call" | custom-call | flops 3221225472 | bytes 1048576 | tf_op jit(solution)/shard_map/pallas_call | solution.py:241
  (1 shorter events, 0.0 us)
Async XLA Ops:
  0.0 36.6 %copy-start.8 = (bf16[4096,48]{0,1:T(8,128)(2,1)S(1)}, bf16[4096,48]{0,1:T(8,128)(2,1)}, u32[]{:S(2)}) copy-start(bf16[4096,48]{0,1:T(8,128)(2,1)} %param.14) | copy-start | bytes 1179652
  39.4 18.3 %all-to-all-start.2 = ((bf16[64,24,128]{2,1,0:T(8,128)(2,1)}), bf16[64,24,128]{2,1,0:T(8,128)(2,1)S(1)}, u32[]{:S(2)}, u32[]{:S(2)}) async-start(bf16[64,24,128]{2,1,0:T(8,128)(2,1)} %get-tuple-element.30), calls=%async_computation.2 | async-start | bytes 786432 | tf_op jit(solution)/shard_map/all_to_all | solution.py:345
  59.1 19.2 %copy-start = (bf16[1024,1024]{1,0:T(8,128)(2,1)S(1)}, bf16[1024,1024]{1,0:T(8,128)(2,1)}, u32[]{:S(2)}) copy-start(bf16[1024,1024]{1,0:T(8,128)(2,1)} %w2_self_ref.1) | copy-start | bytes 6291460
  59.1 19.2 %copy-start.4 = (s32[16,10]{1,0:T(8,128)S(1)}, s32[16,10]{1,0:T(8,128)}, u32[]{:S(2)}) copy-start(s32[16,10]{1,0:T(8,128)} %neighbours_ref.1) | copy-start | bytes 1924
  59.1 19.2 %copy-start.5 = (f32[1024]{0:T(1024)S(1)}, f32[1024]{0:T(1024)}, u32[]{:S(2)}) copy-start(f32[1024]{0:T(1024)} %param.17) | copy-start | bytes 12292
  59.1 19.1 %copy-start.6 = (f32[1024]{0:T(1024)S(1)}, f32[1024]{0:T(1024)}, u32[]{:S(2)}) copy-start(f32[1024]{0:T(1024)} %param.20) | copy-start | bytes 12292
  59.1 19.1 %copy-start.7 = (s32[16]{0:T(128)S(1)}, s32[16]{0:T(128)}, u32[]{:S(2)}) copy-start(s32[16]{0:T(128)} %param.25) | copy-start | bytes 196
  78.3 1.6 %copy-start.1 = (bf16[1024,1024]{1,0:T(8,128)(2,1)S(1)}, bf16[1024,1024]{1,0:T(8,128)(2,1)}, u32[]{:S(2)}) copy-start(bf16[1024,1024]{1,0:T(8,128)(2,1)} %w2_neigh_ref.1) | copy-start | bytes 6291460
  79.9 1.4 %copy-start.2 = (bf16[768,1024]{1,0:T(8,128)(2,1)S(1)}, bf16[768,1024]{1,0:T(8,128)(2,1)}, u32[]{:S(2)}) copy-start(bf16[768,1024]{1,0:T(8,128)(2,1)} %w1_self_ref.1) | copy-start | bytes 4718596
  81.3 1.4 %copy-start.3 = (bf16[768,1024]{1,0:T(8,128)(2,1)S(1)}, bf16[768,1024]{1,0:T(8,128)(2,1)}, u32[]{:S(2)}) copy-start(bf16[768,1024]{1,0:T(8,128)(2,1)} %w1_neigh_ref.1) | copy-start | bytes 4718596

commit v5 on v4

--- a/solution.py
+++ b/solution.py
@@ -27,17 +27,33 @@
     return lax.broadcasted_iota(jnp.int32, shape, dimension)
 
 
-def route_kernel(
-    owner_hbm, row_hbm, count_hbm, request_ref, code_ref, owner_ref, row_ref, count_ref, arrived
-):
-    copies = [
-        pltpu.make_async_copy(source, target, arrived.at[i])
-        for i, (source, target) in enumerate(
-            ((owner_hbm, owner_ref), (row_hbm, row_ref), (count_hbm, count_ref))
-        )
-    ]
+def bring(pairs, arrived):
+    copies = [pltpu.make_async_copy(a, b, arrived.at[i]) for i, (a, b) in enumerate(pairs)]
     for copy in copies:
         copy.start()
+    return copies
+
+
+def route_kernel(
+    owner_hbm,
+    row_hbm,
+    count_hbm,
+    w_self_hbm,
+    w_neigh_hbm,
+    request_ref,
+    code_ref,
+    w_self_ref,
+    w_neigh_ref,
+    owner_ref,
+    row_ref,
+    count_ref,
+    arrived,
+    weights_arrived,
+):
+    copies = bring(
+        ((owner_hbm, owner_ref), (row_hbm, row_ref), (count_hbm, count_ref)), arrived
+    )
+    weights = bring(((w_self_hbm, w_self_ref), (w_neigh_hbm, w_neigh_ref)), weights_arrived)
     for copy in copies:
         copy.wait()
     chunks = owner_ref.shape[0]
@@ -108,6 +124,8 @@
         total[:PEERS] * 64.0 + total[PEERS : 2 * PEERS]
     ).astype(jnp.int32)
     code_ref[:, :CAPACITY] = total[2 * PEERS :]
+    for copy in weights:
+        copy.wait()
 
 
 def spread(slots, scratch):
@@ -128,10 +146,29 @@
     )
 
 
-def find_kernel(asked_ref, features_ref, found_ref, crowded_ref, table, scratch):
+def find_first_kernel(
+    asked_ref,
+    features_ref,
+    w_self_hbm,
+    w_neigh_hbm,
+    found_ref,
+    crowded_ref,
+    w_self_ref,
+    w_neigh_ref,
+    table,
+    scratch,
+    weights_arrived,
+):
+    weights = bring(((w_self_hbm, w_self_ref), (w_neigh_hbm, w_neigh_ref)), weights_arrived)
     asked = asked_ref[:, 0, :]
     crowded_ref[0, 0] = jnp.max(jnp.where(iota(asked.shape, 1) == FLAG, asked, 0))
-    spread(asked, scratch)
+    find_kernel(asked_ref, features_ref, found_ref, table, scratch)
+    for copy in weights:
+        copy.wait()
+
+
+def find_kernel(asked_ref, features_ref, found_ref, table, scratch):
+    spread(asked_ref[:, 0, :], scratch)
     for low in range(LOWS):
         table[low * WIDTH : (low + 1) * WIDTH, :] = features_ref[:, low * HIGH : (low + 1) * HIGH]
     one = jnp.bfloat16(1.0)
@@ -182,22 +219,17 @@
     )
 
 
-def finish(sums, targets):
+def mean_kernel(reply_ref, code_ref, rest_ref, out_ref, scratch):
+    targets = out_ref.shape[0]
+    sums = sums_of(reply_ref, code_ref, scratch, targets) + rest_ref[...]
     own = sums[:targets]
     neigh = sums[targets:]
     mean = neigh / neigh[:, 2 * WIDTH : 2 * WIDTH + 1]
-    return jnp.where(iota(own.shape, 1) < WIDTH, own, mean).astype(jnp.bfloat16)
-
-
-def mean_kernel(reply_ref, code_ref, out_ref, sums_ref, scratch):
-    sums = sums_of(reply_ref, code_ref, scratch, out_ref.shape[0])
-    sums_ref[...] = sums
-    out_ref[...] = finish(sums, out_ref.shape[0])
-
-
-def rest_kernel(reply_ref, code_ref, sums_ref, out_ref, scratch):
-    sums = sums_ref[...] + sums_of(reply_ref, code_ref, scratch, out_ref.shape[0])
-    out_ref[...] = finish(sums, out_ref.shape[0])
+    out_ref[...] = jnp.where(iota(own.shape, 1) < WIDTH, own, mean).astype(jnp.bfloat16)
+
+
+def rest_kernel(reply_ref, code_ref, sums_ref, scratch):
+    sums_ref[...] = sums_of(reply_ref, code_ref, scratch, sums_ref.shape[0] // 2)
 
 
 def layers_kernel(
@@ -237,89 +269,113 @@
     out_ref[...] = (total + bias_two_ref[...]).astype(jnp.bfloat16)
 
 
-def call(kernel, out_shape, scratch_shapes, flops, *operands, space=VMEM, out_specs=None):
+def call(kernel, out_shape, scratch_shapes, flops, *operands, spaces=None, out_spaces=None):
+    spaces = spaces or [VMEM] * len(operands)
+    out_spaces = out_spaces or [VMEM] * len(out_shape)
     return pl.pallas_call(
         kernel,
         out_shape=out_shape,
-        in_specs=[pl.BlockSpec(memory_space=space)] * len(operands),
-        out_specs=out_specs or jax.tree.map(lambda _: pl.BlockSpec(memory_space=VMEM), out_shape),
+        in_specs=[pl.BlockSpec(memory_space=space) for space in spaces],
+        out_specs=[pl.BlockSpec(memory_space=space) for space in out_spaces],
         scratch_shapes=scratch_shapes,
         compiler_params=pltpu.CompilerParams(vmem_limit_bytes=LIMIT),
         cost_estimate=pl.CostEstimate(flops=flops, bytes_accessed=1 << 20, transcendentals=0),
     )(*operands)
 
 
-def route(owner, row_index, count_one):
+def in_hbm(*arrays):
+    return [pltpu.with_memory_space_constraint(a, pltpu.HBM) for a in arrays]
+
+
+def in_vmem(*arrays):
+    return [pltpu.VMEM(a.shape, a.dtype) for a in arrays]
+
+
+def route(owner, row_index, count_one, weights):
     lines = owner.shape[0] // LANES
     return call(
         route_kernel,
         [
             jax.ShapeDtypeStruct((PEERS, 1, LANES), jnp.int32),
             jax.ShapeDtypeStruct((PEERS, LANES), jnp.float32),
+            *in_vmem(*weights),
         ],
         [
             pltpu.VMEM((lines, LANES), jnp.int32),
             pltpu.VMEM((lines, LANES), jnp.int32),
             pltpu.VMEM((count_one.shape[0] // LANES, LANES), jnp.int32),
             pltpu.SemaphoreType.DMA((3,)),
+            pltpu.SemaphoreType.DMA((2,)),
         ],
         1 << 30,
-        *[
-            pltpu.with_memory_space_constraint(a.reshape(-1, LANES), pltpu.HBM)
-            for a in (owner, row_index, count_one)
+        *in_hbm(*[a.reshape(-1, LANES) for a in (owner, row_index, count_one)], *weights),
+        spaces=[pltpu.HBM] * 5,
+    )
+
+
+def find_scratch():
+    return [
+        pltpu.VMEM((LOWS * WIDTH, HIGH), jnp.bfloat16),
+        pltpu.VMEM((PEERS, LANES), jnp.int32),
+    ]
+
+
+def find_first(asked, features, weights):
+    return call(
+        find_first_kernel,
+        [
+            pltpu.VMEM((PEERS, PART, LANES), jnp.bfloat16),
+            pltpu.SMEM((1, 1), jnp.int32),
+            *in_vmem(*weights),
         ],
-        space=pltpu.HBM,
-    )
-
-
-def find(asked, features):
-    return call(
-        find_kernel,
-        [
-            jax.ShapeDtypeStruct((PEERS, PART, LANES), jnp.bfloat16),
-            jax.ShapeDtypeStruct((1, 1), jnp.int32),
-        ],
-        [
-            pltpu.VMEM((LOWS * WIDTH, HIGH), jnp.bfloat16),
-            pltpu.VMEM((PEERS, LANES), jnp.int32),
-        ],
+        [*find_scratch(), pltpu.SemaphoreType.DMA((2,))],
         5 << 30,
         asked,
         features.T,
-        out_specs=[pl.BlockSpec(memory_space=VMEM), pl.BlockSpec(memory_space=pltpu.SMEM)],
-    )
-
-
-def means(replies, code, targets):
+        *in_hbm(*weights),
+        spaces=[VMEM, VMEM, pltpu.HBM, pltpu.HBM],
+        out_spaces=[VMEM, pltpu.SMEM, VMEM, VMEM],
+    )
+
+
+def find(asked, features):
+    return call(
+        find_kernel,
+        [jax.ShapeDtypeStruct((PEERS, PART, LANES), jnp.bfloat16)],
+        find_scratch(),
+        5 << 30,
+        asked,
+        features.T,
+    )[0]
+
+
+def means(replies, code, rest):
     return call(
         mean_kernel,
-        [
-            jax.ShapeDtypeStruct((targets, LANES), jnp.bfloat16),
-            jax.ShapeDtypeStruct((2 * targets, LANES), jnp.float32),
-        ],
+        [jax.ShapeDtypeStruct((rest.shape[0] // 2, LANES), jnp.bfloat16)],
         [pltpu.VMEM((PEERS, LANES), jnp.float32)],
         4 << 30,
         replies,
         code,
-    )
-
-
-def with_rest(replies, code, sums, targets):
+        rest,
+    )[0]
+
+
+def rest_sums(replies, code, targets):
     return call(
         rest_kernel,
-        jax.ShapeDtypeStruct((targets, LANES), jnp.bfloat16),
+        [jax.ShapeDtypeStruct((2 * targets, LANES), jnp.float32)],
         [pltpu.VMEM((PEERS, LANES), jnp.float32)],
         4 << 30,
         replies,
         code,
-        sums,
-    )
+    )[0]
 
 
 def layers(parts, w1_self, w1_neigh, bias_one, w2_self, w2_neigh, bias_two, neighbours, count):
     return call(
         layers_kernel,
-        jax.ShapeDtypeStruct((BLOCK, w2_self.shape[1]), jnp.bfloat16),
+        [jax.ShapeDtypeStruct((BLOCK, w2_self.shape[1]), jnp.bfloat16)],
         [],
         3 << 30,
         parts,
@@ -331,7 +387,7 @@
         bias_two.reshape(1, -1),
         neighbours,
         count.reshape(1, -1),
-    )
+    )[0]
 
 
 def later_slots(slots):
@@ -360,19 +416,19 @@
     count_two,
 ):
     targets = count_one.shape[0]
-    requests, code = route(owner, row_index, count_one)
+    requests, code, w1_self, w1_neigh = route(owner, row_index, count_one, (w1_self, w1_neigh))
     asked = exchange(requests, "rows")
-    found, crowded = find(asked, features)
-    mine, sums = means(exchange(found, "rows"), code, targets)
-
-    def more(asked, features, code, sums, mine):
-        found, _ = find(later_slots(asked), features)
-        return with_rest(exchange(found, "rows"), later_slots(code), sums, targets)
-
-    def no_more(asked, features, code, sums, mine):
-        return mine
-
-    mine = lax.cond(crowded[0, 0] > 0, more, no_more, asked, features, code, sums, mine)
+    found, crowded, w2_self, w2_neigh = find_first(asked, features, (w2_self, w2_neigh))
+
+    def more(asked, features, code):
+        found = find(later_slots(asked), features)
+        return rest_sums(exchange(found, "rows"), later_slots(code), targets)
+
+    def no_more(asked, features, code):
+        return jnp.zeros((2 * targets, LANES), jnp.float32)
+
+    rest = lax.cond(crowded[0, 0] > 0, more, no_more, asked, features, code)
+    mine = means(exchange(found, "rows"), code, rest)
     parts = exchange(mine.reshape(-1, BLOCK, LANES), "feat")
     return layers(
         parts, w1_self, w1_neigh, bias_one, w2_self, w2_neigh, bias_two, neighbours_two, count_two

time: 84.9 us -> 84.1 us (level)
  starting transfers between devices: 4.64 us -> 24 us
  blocking collectives: 53.7 us -> 36.5 us
  waiting for transfers between devices: 13 us -> 10.8 us
    all_to_all x1, starting transfers between devices: 4.64 us -> 24 us  [exchange(): return lax.all_to_all(array, axis, split_axis=0, concat_axis=0, tiled=True)]
    all_to_all x2, blocking collectives: 53.7 us -> 36.5 us  [exchange(): return lax.all_to_all(array, axis, split_axis=0, concat_axis=0, tiled=True)]
    all_to_all x1, waiting for transfers between devices: 13 us -> 10.8 us  [exchange(): return lax.all_to_all(array, axis, split_axis=0, concat_axis=0, tiled=True)]
    unnamed x18 -> x22, local copies, waits for them, and re-layouts: 4.44 us -> 3.86 us
where the time goes in v5:
time: 84.1 us; the launch traced here: 83.9 us
  blocking collectives  36.5 us (43%)
  starting transfers between devices  24 us (29%)
  waiting for transfers between devices  10.8 us (13%)
  Pallas kernels  8.64 us (10%)
  local copies, waits for them, and re-layouts  3.88 us (5%)
    all_to_all x2, blocking collectives, exchange(): return lax.all_to_all(array, axis, split_axis=0, concat_axis=0, tiled=True)  36.5 us
    all_to_all x1, starting transfers between devices, exchange(): return lax.all_to_all(array, axis, split_axis=0, concat_axis=0, tiled=True)  24 us
    all_to_all x1, waiting for transfers between devices, exchange(): return lax.all_to_all(array, axis, split_axis=0, concat_axis=0, tiled=True)  10.8 us
    pallas_call x4, Pallas kernels, call(): pl.pallas_call(kernel, out_shape=out_shape, in_specs=[pl.BlockSpec(memory...  8.64 us
    unnamed x22, local copies, waits for them, and re-layouts  3.86 us
  transfers between devices with their start and end apart: 1, of which 1 were waited for; matrix products, arithmetic and copies ran while one was open for 0% of the time, Pallas kernels for 0%

profile of v5, /device:TPU:1, one launch (start us, length us, event | category | flops | bytes accessed | tf_op | source)
XLA Modules:
  0.0 83.9 jit_solution(15750981055817442646)
XLA Ops:
  0.0 0.0 copy-start.10
  0.0 3.1 %shard_map.118 = (s32[64,1,128]{2,1,0:T(1,128)}, f32[64,128]{1,0:T(8,128)S(1)}, bf16[768,1024]{1,0:T(8,128)(2,1)S(1)}, bf16[768,1024]{1,0:T(8,128)(2,1)S(1)}) custom-call(s32[32,128]{1,0:T(8,128)} %bitcast.16, s32[32,128]{1,0:T(8,128)} %bitcast.17, s32[2,128]{1,0:T(2,128)} %bitcast.18, bf16[768,1024]{1,0:T(8,128)(2,1)} %w_self_hbm.2, ...), custom_call_target="tpu_custom_call" | custom-call | flops 1073741824 | bytes 1048576 | tf_op jit(solution)/shard_map/pallas_call | solution.py:275
  3.1 0.0 copy-start.4
  3.2 1.2 %copy-done.4 = bf16[768,1024]{1,0:T(8,128)(2,1)} copy-done((bf16[768,1024]{1,0:T(8,128)(2,1)}, bf16[768,1024]{1,0:T(8,128)(2,1)S(1)}, u32[]{:S(2)}) %copy-start.4) | copy-done | bytes 1572888
  4.3 24.0 %all-to-all-start.1 = ((s32[64,1,128]{2,1,0:T(1,128)}), s32[64,1,128]{2,1,0:T(1,128)S(1)}, u32[]{:S(2)}, u32[]{:S(2)}) async-start(s32[64,1,128]{2,1,0:T(1,128)} %get-tuple-element.25), calls=%async_computation.1 | async-start | bytes 65536 | tf_op jit(solution)/shard_map/all_to_all | solution.py:401
  28.3 10.8 %all-to-all-done.1.asked_ref = s32[64,1,128]{2,1,0:T(1,128)S(1)} async-done(((s32[64,1,128]{2,1,0:T(1,128)}), s32[64,1,128]{2,1,0:T(1,128)S(1)}, u32[]{:S(2)}, u32[]{:S(2)}) %all-to-all-start.1) | async-done | bytes 32800 | tf_op jit(solution)/shard_map/all_to_all | solution.py:401
  39.1 0.0 copy-done.10
  39.1 2.2 %shard_map.119 = (bf16[64,24,128]{2,1,0:T(8,128)(2,1)S(1)}, s32[1,1]{1,0:T(1,128)S(4)}, bf16[1024,1024]{1,0:T(8,128)(2,1)S(1)}, bf16[1024,1024]{1,0:T(8,128)(2,1)S(1)}) custom-call(s32[64,1,128]{2,1,0:T(1,128)S(1)} %all-to-all-done.1.asked_ref, bf16[48,4096]{1,0:T(8,128)(2,1)S(1)} %bitcast.14, bf16[1024,1024]{1,0:T(8,128)(2,1)} %w_self_hbm.3, ...), custom_call_target="tpu_custom_call" | custom-call | flops 5368709120 | bytes 1048576 | tf_op jit(solution)/shard_map/pallas_call | solution.py:275
  41.3 0.0 copy-start.6
  41.3 1.3 %copy-done.6 = bf16[1024,1024]{1,0:T(8,128)(2,1)} copy-done((bf16[1024,1024]{1,0:T(8,128)(2,1)}, bf16[1024,1024]{1,0:T(8,128)(2,1)S(1)}, u32[]{:S(2)}) %copy-start.6) | copy-done | bytes 2097176
  42.7 0.0 copy-start.8
  42.7 1.3 %copy-done.8 = bf16[1024,1024]{1,0:T(8,128)(2,1)} copy-done((bf16[1024,1024]{1,0:T(8,128)(2,1)}, bf16[1024,1024]{1,0:T(8,128)(2,1)S(1)}, u32[]{:S(2)}) %copy-start.8) | copy-done | bytes 2097176
  44.0 17.4 %all_to_all.19.reply_ref = bf16[64,24,128]{2,1,0:T(8,128)(2,1)S(1)} all-to-all(bf16[64,24,128]{2,1,0:T(8,128)(2,1)S(1)} %get-tuple-element.26), channel_id=1, replica_groups=mesh['rows'=64,'feat'=16] {'rows'}, dimensions={0} | all-to-all | bytes 786432 | tf_op jit(solution)/shard_map/all_to_all | solution.py:401
  61.4 0.0 copy-start
  61.4 0.0 copy-start.1
  61.4 0.0 copy-start.2
  61.4 0.0 copy-start.3
  61.4 0.0 copy-start.5
  61.5 0.0 copy-start.7
  61.5 0.0 copy-start.9
  61.5 1.4 %shard_map.120 = bf16[256,128]{1,0:T(8,128)(2,1)S(1)} custom-call(bf16[64,24,128]{2,1,0:T(8,128)(2,1)S(1)} %all_to_all.19.reply_ref, f32[64,128]{1,0:T(8,128)S(1)} %get-tuple-element.27.code_ref, f32[512,128]{1,0:T(8,128)S(1)} %get-tuple-element.37.rest_ref), custom_call_target="tpu_custom_call" | custom-call | flops 4294967296 | bytes 1048576 | tf_op jit(solution)/shard_map/pallas_call | solution.py:275
  62.9 19.1 %all_to_all.20.part_ref = bf16[16,16,128]{2,1,0:T(8,128)(2,1)S(1)} all-to-all(bf16[16,16,128]{2,1,0:T(8,128)(2,1)S(1)} %bitcast.10), channel_id=1, replica_groups=mesh['rows'=64,'feat'=16] {'feat'}, dimensions={0} | all-to-all | bytes 131072 | tf_op jit(solution)/shard_map/all_to_all | solution.py:401
  82.0 0.0 copy-done
  82.0 0.0 copy-done.1
  82.0 0.0 copy-done.2
  82.0 0.0 copy-done.3
  82.0 0.0 copy-done.5
  82.0 0.0 copy-done.7
  82.0 0.0 copy-done.9
  82.0 1.9 %shard_map.121 = bf16[16,1024]{1,0:T(8,128)(2,1)} custom-call(bf16[16,16,128]{2,1,0:T(8,128)(2,1)S(1)} %all_to_all.20.part_ref, bf16[768,1024]{1,0:T(8,128)(2,1)S(1)} %get-tuple-element.29.w1_self_ref, bf16[768,1024]{1,0:T(8,128)(2,1)S(1)} %copy-done.5, f32[1,1024]{1,0:T(1,128)S(1)} %bitcast.11, bf16[1024,1024]{1,0:T(8,128)(2,1)S(1)} %copy-done.7, ...), custom_call_target="tpu_custom_call" | custom-call | flops 3221225472 | bytes 1048576 | tf_op jit(solution)/shard_map/pallas_call | solution.py:275
  (2 shorter events, 0.0 us)
Async XLA Ops:
  0.0 39.1 %copy-start.10 = (bf16[4096,48]{0,1:T(8,128)(2,1)S(1)}, bf16[4096,48]{0,1:T(8,128)(2,1)}, u32[]{:S(2)}) copy-start(bf16[4096,48]{0,1:T(8,128)(2,1)} %param.14) | copy-start | bytes 1179652
  3.1 1.2 %copy-start.4 = (bf16[768,1024]{1,0:T(8,128)(2,1)}, bf16[768,1024]{1,0:T(8,128)(2,1)S(1)}, u32[]{:S(2)}) copy-start(bf16[768,1024]{1,0:T(8,128)(2,1)S(1)} %get-tuple-element.30.w1_neigh_ref) | copy-start | bytes 4718596
  4.3 34.7 %all-to-all-start.1 = ((s32[64,1,128]{2,1,0:T(1,128)}), s32[64,1,128]{2,1,0:T(1,128)S(1)}, u32[]{:S(2)}, u32[]{:S(2)}) async-start(s32[64,1,128]{2,1,0:T(1,128)} %get-tuple-element.25), calls=%async_computation.1 | async-start | bytes 65536 | tf_op jit(solution)/shard_map/all_to_all | solution.py:401
  41.3 1.3 %copy-start.6 = (bf16[1024,1024]{1,0:T(8,128)(2,1)}, bf16[1024,1024]{1,0:T(8,128)(2,1)S(1)}, u32[]{:S(2)}) copy-start(bf16[1024,1024]{1,0:T(8,128)(2,1)S(1)} %get-tuple-element.31.w2_self_ref) | copy-start | bytes 6291460
  42.7 1.3 %copy-start.8 = (bf16[1024,1024]{1,0:T(8,128)(2,1)}, bf16[1024,1024]{1,0:T(8,128)(2,1)S(1)}, u32[]{:S(2)}) copy-start(bf16[1024,1024]{1,0:T(8,128)(2,1)S(1)} %get-tuple-element.32.w2_neigh_ref) | copy-start | bytes 6291460
  61.4 20.5 %copy-start = (s32[16,10]{1,0:T(8,128)S(1)}, s32[16,10]{1,0:T(8,128)}, u32[]{:S(2)}) copy-start(s32[16,10]{1,0:T(8,128)} %neighbours_ref.1) | copy-start | bytes 1924
  61.4 20.5 %copy-start.1 = (f32[1024]{0:T(1024)S(1)}, f32[1024]{0:T(1024)}, u32[]{:S(2)}) copy-start(f32[1024]{0:T(1024)} %param.17) | copy-start | bytes 12292
  61.4 20.5 %copy-start.2 = (f32[1024]{0:T(1024)S(1)}, f32[1024]{0:T(1024)}, u32[]{:S(2)}) copy-start(f32[1024]{0:T(1024)} %param.20) | copy-start | bytes 12292
  61.4 20.5 %copy-start.3 = (s32[16]{0:T(128)S(1)}, s32[16]{0:T(128)}, u32[]{:S(2)}) copy-start(s32[16]{0:T(128)} %param.25) | copy-start | bytes 196
  61.4 20.6 %copy-start.5 = (bf16[768,1024]{1,0:T(8,128)(2,1)S(1)}, bf16[768,1024]{1,0:T(8,128)(2,1)}, u32[]{:S(2)}) copy-start(bf16[768,1024]{1,0:T(8,128)(2,1)} %copy-done.4) | copy-start | bytes 4718596
  61.5 20.6 %copy-start.7 = (bf16[1024,1024]{1,0:T(8,128)(2,1)S(1)}, bf16[1024,1024]{1,0:T(8,128)(2,1)}, u32[]{:S(2)}) copy-start(bf16[1024,1024]{1,0:T(8,128)(2,1)} %copy-done.6) | copy-start | bytes 6291460
  61.5 20.6 %copy-start.9 = (bf16[1024,1024]{1,0:T(8,128)(2,1)S(1)}, bf16[1024,1024]{1,0:T(8,128)(2,1)}, u32[]{:S(2)}) copy-start(bf16[1024,1024]{1,0:T(8,128)(2,1)} %copy-done.8) | copy-start | bytes 6291460

commit v6 on v5

--- a/solution.py
+++ b/solution.py
@@ -27,33 +27,17 @@
     return lax.broadcasted_iota(jnp.int32, shape, dimension)
 
 
-def bring(pairs, arrived):
-    copies = [pltpu.make_async_copy(a, b, arrived.at[i]) for i, (a, b) in enumerate(pairs)]
+def route_kernel(
+    owner_hbm, row_hbm, count_hbm, request_ref, code_ref, owner_ref, row_ref, count_ref, arrived
+):
+    copies = [
+        pltpu.make_async_copy(source, target, arrived.at[i])
+        for i, (source, target) in enumerate(
+            ((owner_hbm, owner_ref), (row_hbm, row_ref), (count_hbm, count_ref))
+        )
+    ]
     for copy in copies:
         copy.start()
-    return copies
-
-
-def route_kernel(
-    owner_hbm,
-    row_hbm,
-    count_hbm,
-    w_self_hbm,
-    w_neigh_hbm,
-    request_ref,
-    code_ref,
-    w_self_ref,
-    w_neigh_ref,
-    owner_ref,
-    row_ref,
-    count_ref,
-    arrived,
-    weights_arrived,
-):
-    copies = bring(
-        ((owner_hbm, owner_ref), (row_hbm, row_ref), (count_hbm, count_ref)), arrived
-    )
-    weights = bring(((w_self_hbm, w_self_ref), (w_neigh_hbm, w_neigh_ref)), weights_arrived)
     for copy in copies:
         copy.wait()
     chunks = owner_ref.shape[0]
@@ -124,8 +108,6 @@
         total[:PEERS] * 64.0 + total[PEERS : 2 * PEERS]
     ).astype(jnp.int32)
     code_ref[:, :CAPACITY] = total[2 * PEERS :]
-    for copy in weights:
-        copy.wait()
 
 
 def spread(slots, scratch):
@@ -146,25 +128,10 @@
     )
 
 
-def find_first_kernel(
-    asked_ref,
-    features_ref,
-    w_self_hbm,
-    w_neigh_hbm,
-    found_ref,
-    crowded_ref,
-    w_self_ref,
-    w_neigh_ref,
-    table,
-    scratch,
-    weights_arrived,
-):
-    weights = bring(((w_self_hbm, w_self_ref), (w_neigh_hbm, w_neigh_ref)), weights_arrived)
+def find_first_kernel(asked_ref, features_ref, found_ref, crowded_ref, table, scratch):
     asked = asked_ref[:, 0, :]
     crowded_ref[0, 0] = jnp.max(jnp.where(iota(asked.shape, 1) == FLAG, asked, 0))
     find_kernel(asked_ref, features_ref, found_ref, table, scratch)
-    for copy in weights:
-        copy.wait()
 
 
 def find_kernel(asked_ref, features_ref, found_ref, table, scratch):
@@ -283,33 +250,26 @@
     )(*operands)
 
 
-def in_hbm(*arrays):
-    return [pltpu.with_memory_space_constraint(a, pltpu.HBM) for a in arrays]
-
-
-def in_vmem(*arrays):
-    return [pltpu.VMEM(a.shape, a.dtype) for a in arrays]
-
-
-def route(owner, row_index, count_one, weights):
+def route(owner, row_index, count_one):
     lines = owner.shape[0] // LANES
     return call(
         route_kernel,
         [
             jax.ShapeDtypeStruct((PEERS, 1, LANES), jnp.int32),
             jax.ShapeDtypeStruct((PEERS, LANES), jnp.float32),
-            *in_vmem(*weights),
         ],
         [
             pltpu.VMEM((lines, LANES), jnp.int32),
             pltpu.VMEM((lines, LANES), jnp.int32),
             pltpu.VMEM((count_one.shape[0] // LANES, LANES), jnp.int32),
             pltpu.SemaphoreType.DMA((3,)),
-            pltpu.SemaphoreType.DMA((2,)),
         ],
         1 << 30,
-        *in_hbm(*[a.reshape(-1, LANES) for a in (owner, row_index, count_one)], *weights),
-        spaces=[pltpu.HBM] * 5,
+        *[
+            pltpu.with_memory_space_constraint(a.reshape(-1, LANES), pltpu.HBM)
+            for a in (owner, row_index, count_one)
+        ],
+        spaces=[pltpu.HBM] * 3,
     )
 
 
@@ -320,21 +280,18 @@
     ]
 
 
-def find_first(asked, features, weights):
+def find_first(asked, features):
     return call(
         find_first_kernel,
         [
             pltpu.VMEM((PEERS, PART, LANES), jnp.bfloat16),
             pltpu.SMEM((1, 1), jnp.int32),
-            *in_vmem(*weights),
         ],
-        [*find_scratch(), pltpu.SemaphoreType.DMA((2,))],
+        find_scratch(),
         5 << 30,
         asked,
         features.T,
-        *in_hbm(*weights),
-        spaces=[VMEM, VMEM, pltpu.HBM, pltpu.HBM],
-        out_spaces=[VMEM, pltpu.SMEM, VMEM, VMEM],
+        out_spaces=[VMEM, pltpu.SMEM],
     )
 
 
@@ -416,9 +373,9 @@
     count_two,
 ):
     targets = count_one.shape[0]
-    requests, code, w1_self, w1_neigh = route(owner, row_index, count_one, (w1_self, w1_neigh))
+    requests, code = route(owner, row_index, count_one)
     asked = exchange(requests, "rows")
-    found, crowded, w2_self, w2_neigh = find_first(asked, features, (w2_self, w2_neigh))
+    found, crowded = find_first(asked, features)
 
     def more(asked, features, code):
         found = find(later_slots(asked), features)

time: 84.1 us -> 79.6 us (0.946)
  local copies, waits for them, and re-layouts: 3.88 us -> 0.06 us
    unnamed x22 -> x18, local copies, waits for them, and re-layouts: 3.86 us -> 0.04 us
where the time goes in v6:
time: 79.6 us; the launch traced here: 79.3 us
  blocking collectives  36.5 us (46%)
  starting transfers between devices  24 us (30%)
  waiting for transfers between devices  10.8 us (14%)
  Pallas kernels  7.87 us (10%)
    all_to_all x2, blocking collectives, exchange(): return lax.all_to_all(array, axis, split_axis=0, concat_axis=0, tiled=True)  36.5 us
    all_to_all x1, starting transfers between devices, exchange(): return lax.all_to_all(array, axis, split_axis=0, concat_axis=0, tiled=True)  24 us
    all_to_all x1, waiting for transfers between devices, exchange(): return lax.all_to_all(array, axis, split_axis=0, concat_axis=0, tiled=True)  10.8 us
    pallas_call x4, Pallas kernels, call(): pl.pallas_call(kernel, out_shape=out_shape, in_specs=[pl.BlockSpec(memory...  7.87 us
  transfers between devices with their start and end apart: 1, of which 1 were waited for; matrix products, arithmetic and copies ran while one was open for 0% of the time, Pallas kernels for 0%

profile of v6, /device:TPU:1, one launch (start us, length us, event | category | flops | bytes accessed | tf_op | source)
XLA Modules:
  0.0 79.3 jit_solution(2544555660796471335)
XLA Ops:
  0.0 0.0 copy-start.8
  0.0 2.6 %shard_map.118 = (s32[64,1,128]{2,1,0:T(1,128)}, f32[64,128]{1,0:T(8,128)S(1)}) custom-call(s32[32,128]{1,0:T(8,128)} %bitcast.16, s32[32,128]{1,0:T(8,128)} %bitcast.17, s32[2,128]{1,0:T(2,128)} %bitcast.18), custom_call_target="tpu_custom_call" | custom-call | flops 1073741824 | bytes 1048576 | tf_op jit(solution)/shard_map/pallas_call | solution.py:242
  2.6 24.0 %all-to-all-start.1 = ((s32[64,1,128]{2,1,0:T(1,128)}), s32[64,1,128]{2,1,0:T(1,128)S(1)}, u32[]{:S(2)}, u32[]{:S(2)}) async-start(s32[64,1,128]{2,1,0:T(1,128)} %get-tuple-element.21), calls=%async_computation.1 | async-start | bytes 65536 | tf_op jit(solution)/shard_map/all_to_all | solution.py:358
  26.6 10.8 %all-to-all-done.1.asked_ref = s32[64,1,128]{2,1,0:T(1,128)S(1)} async-done(((s32[64,1,128]{2,1,0:T(1,128)}), s32[64,1,128]{2,1,0:T(1,128)S(1)}, u32[]{:S(2)}, u32[]{:S(2)}) %all-to-all-start.1) | async-done | bytes 32800 | tf_op jit(solution)/shard_map/all_to_all | solution.py:358
  37.4 0.0 copy-done.8
  37.4 2.0 %shard_map.119 = (bf16[64,24,128]{2,1,0:T(8,128)(2,1)S(1)}, s32[1,1]{1,0:T(1,128)S(4)}) custom-call(s32[64,1,128]{2,1,0:T(1,128)S(1)} %all-to-all-done.1.asked_ref, bf16[48,4096]{1,0:T(8,128)(2,1)S(1)} %bitcast.14), custom_call_target="tpu_custom_call" | custom-call | flops 5368709120 | bytes 1048576 | tf_op jit(solution)/shard_map/pallas_call | solution.py:242
  39.4 17.4 %all_to_all.19.reply_ref = bf16[64,24,128]{2,1,0:T(8,128)(2,1)S(1)} all-to-all(bf16[64,24,128]{2,1,0:T(8,128)(2,1)S(1)} %get-tuple-element.22), channel_id=1, replica_groups=mesh['rows'=64,'feat'=16] {'rows'}, dimensions={0} | all-to-all | bytes 786432 | tf_op jit(solution)/shard_map/all_to_all | solution.py:358
  56.9 0.0 copy-start
  56.9 0.0 copy-start.1
  56.9 0.0 copy-start.2
  56.9 0.0 copy-start.3
  56.9 0.0 copy-start.4
  56.9 0.0 copy-start.5
  56.9 0.0 copy-start.6
  56.9 0.0 copy-start.7
  56.9 1.4 %shard_map.120 = bf16[256,128]{1,0:T(8,128)(2,1)S(1)} custom-call(bf16[64,24,128]{2,1,0:T(8,128)(2,1)S(1)} %all_to_all.19.reply_ref, f32[64,128]{1,0:T(8,128)S(1)} %get-tuple-element.23.code_ref, f32[512,128]{1,0:T(8,128)S(1)} %get-tuple-element.29.rest_ref), custom_call_target="tpu_custom_call" | custom-call | flops 4294967296 | bytes 1048576 | tf_op jit(solution)/shard_map/pallas_call | solution.py:242
  58.3 19.1 %all_to_all.20.part_ref = bf16[16,16,128]{2,1,0:T(8,128)(2,1)S(1)} all-to-all(bf16[16,16,128]{2,1,0:T(8,128)(2,1)S(1)} %bitcast.10), channel_id=1, replica_groups=mesh['rows'=64,'feat'=16] {'feat'}, dimensions={0} | all-to-all | bytes 131072 | tf_op jit(solution)/shard_map/all_to_all | solution.py:358
  77.4 0.0 copy-done
  77.4 0.0 copy-done.1
  77.4 0.0 copy-done.2
  77.4 0.0 copy-done.3
  77.4 0.0 copy-done.4
  77.4 0.0 copy-done.5
  77.4 0.0 copy-done.6
  77.5 0.0 copy-done.7
  77.5 1.9 %shard_map.121 = bf16[16,1024]{1,0:T(8,128)(2,1)} custom-call(bf16[16,16,128]{2,1,0:T(8,128)(2,1)S(1)} %all_to_all.20.part_ref, bf16[768,1024]{1,0:T(8,128)(2,1)S(1)} %copy-done.2, bf16[768,1024]{1,0:T(8,128)(2,1)S(1)} %copy-done.3, f32[1,1024]{1,0:T(1,128)S(1)} %bitcast.11, bf16[1024,1024]{1,0:T(8,128)(2,1)S(1)} %copy-done, ...), custom_call_target="tpu_custom_call" | custom-call | flops 3221225472 | bytes 1048576 | tf_op jit(solution)/shard_map/pallas_call | solution.py:242
  (2 shorter events, 0.1 us)
Async XLA Ops:
  0.0 37.4 %copy-start.8 = (bf16[4096,48]{0,1:T(8,128)(2,1)S(1)}, bf16[4096,48]{0,1:T(8,128)(2,1)}, u32[]{:S(2)}) copy-start(bf16[4096,48]{0,1:T(8,128)(2,1)} %param.14) | copy-start | bytes 1179652
  2.6 34.7 %all-to-all-start.1 = ((s32[64,1,128]{2,1,0:T(1,128)}), s32[64,1,128]{2,1,0:T(1,128)S(1)}, u32[]{:S(2)}, u32[]{:S(2)}) async-start(s32[64,1,128]{2,1,0:T(1,128)} %get-tuple-element.21), calls=%async_computation.1 | async-start | bytes 65536 | tf_op jit(solution)/shard_map/all_to_all | solution.py:358
  56.9 20.6 %copy-start = (bf16[1024,1024]{1,0:T(8,128)(2,1)S(1)}, bf16[1024,1024]{1,0:T(8,128)(2,1)}, u32[]{:S(2)}) copy-start(bf16[1024,1024]{1,0:T(8,128)(2,1)} %w2_self_ref.1) | copy-start | bytes 6291460
  56.9 20.6 %copy-start.1 = (bf16[1024,1024]{1,0:T(8,128)(2,1)S(1)}, bf16[1024,1024]{1,0:T(8,128)(2,1)}, u32[]{:S(2)}) copy-start(bf16[1024,1024]{1,0:T(8,128)(2,1)} %w2_neigh_ref.1) | copy-start | bytes 6291460
  56.9 20.6 %copy-start.2 = (bf16[768,1024]{1,0:T(8,128)(2,1)S(1)}, bf16[768,1024]{1,0:T(8,128)(2,1)}, u32[]{:S(2)}) copy-start(bf16[768,1024]{1,0:T(8,128)(2,1)} %w1_self_ref.1) | copy-start | bytes 4718596
  56.9 20.6 %copy-start.3 = (bf16[768,1024]{1,0:T(8,128)(2,1)S(1)}, bf16[768,1024]{1,0:T(8,128)(2,1)}, u32[]{:S(2)}) copy-start(bf16[768,1024]{1,0:T(8,128)(2,1)} %w1_neigh_ref.1) | copy-start | bytes 4718596
  56.9 20.6 %copy-start.4 = (s32[16,10]{1,0:T(8,128)S(1)}, s32[16,10]{1,0:T(8,128)}, u32[]{:S(2)}) copy-start(s32[16,10]{1,0:T(8,128)} %neighbours_ref.1) | copy-start | bytes 1924
  56.9 20.6 %copy-start.5 = (f32[1024]{0:T(1024)S(1)}, f32[1024]{0:T(1024)}, u32[]{:S(2)}) copy-start(f32[1024]{0:T(1024)} %param.17) | copy-start | bytes 12292
  56.9 20.6 %copy-start.6 = (f32[1024]{0:T(1024)S(1)}, f32[1024]{0:T(1024)}, u32[]{:S(2)}) copy-start(f32[1024]{0:T(1024)} %param.20) | copy-start | bytes 12292
  56.9 20.6 %copy-start.7 = (s32[16]{0:T(128)S(1)}, s32[16]{0:T(128)}, u32[]{:S(2)}) copy-start(s32[16]{0:T(128)} %param.25) | copy-start | bytes 196

commit v7 on v6

--- a/solution.py
+++ b/solution.py
@@ -255,7 +255,7 @@
     return call(
         route_kernel,
         [
-            jax.ShapeDtypeStruct((PEERS, 1, LANES), jnp.int32),
+            pltpu.VMEM((PEERS, 1, LANES), jnp.int32),
             jax.ShapeDtypeStruct((PEERS, LANES), jnp.float32),
         ],
         [

time: 79.6 us -> 79.6 us (level)
  no operation moved by 1% of the time
where the time goes in v7:
time: 79.6 us; the launch traced here: 79.3 us
  blocking collectives  36.5 us (46%)
  starting transfers between devices  24 us (30%)
  waiting for transfers between devices  10.8 us (14%)
  Pallas kernels  7.87 us (10%)
    all_to_all x2, blocking collectives, exchange(): return lax.all_to_all(array, axis, split_axis=0, concat_axis=0, tiled=True)  36.5 us
    all_to_all x1, starting transfers between devices, exchange(): return lax.all_to_all(array, axis, split_axis=0, concat_axis=0, tiled=True)  24 us
    all_to_all x1, waiting for transfers between devices, exchange(): return lax.all_to_all(array, axis, split_axis=0, concat_axis=0, tiled=True)  10.8 us
    pallas_call x4, Pallas kernels, call(): pl.pallas_call(kernel, out_shape=out_shape, in_specs=[pl.BlockSpec(memory...  7.87 us
  transfers between devices with their start and end apart: 1, of which 1 were waited for; matrix products, arithmetic and copies ran while one was open for 0% of the time, Pallas kernels for 0%

profile of v7, /device:TPU:1, one launch (start us, length us, event | category | flops | bytes accessed | tf_op | source)
XLA Modules:
  0.0 79.3 jit_solution(2544555660796471335)
XLA Ops:
  0.0 0.0 copy-start.8
  0.0 2.6 %shard_map.118 = (s32[64,1,128]{2,1,0:T(1,128)}, f32[64,128]{1,0:T(8,128)S(1)}) custom-call(s32[32,128]{1,0:T(8,128)} %bitcast.16, s32[32,128]{1,0:T(8,128)} %bitcast.17, s32[2,128]{1,0:T(2,128)} %bitcast.18), custom_call_target="tpu_custom_call" | custom-call | flops 1073741824 | bytes 1048576 | tf_op jit(solution)/shard_map/pallas_call | solution.py:242
  2.6 24.0 %all-to-all-start.1 = ((s32[64,1,128]{2,1,0:T(1,128)}), s32[64,1,128]{2,1,0:T(1,128)S(1)}, u32[]{:S(2)}, u32[]{:S(2)}) async-start(s32[64,1,128]{2,1,0:T(1,128)} %get-tuple-element.21), calls=%async_computation.1 | async-start | bytes 65536 | tf_op jit(solution)/shard_map/all_to_all | solution.py:358
  26.6 10.8 %all-to-all-done.1.asked_ref = s32[64,1,128]{2,1,0:T(1,128)S(1)} async-done(((s32[64,1,128]{2,1,0:T(1,128)}), s32[64,1,128]{2,1,0:T(1,128)S(1)}, u32[]{:S(2)}, u32[]{:S(2)}) %all-to-all-start.1) | async-done | bytes 32800 | tf_op jit(solution)/shard_map/all_to_all | solution.py:358
  37.4 0.0 copy-done.8
  37.4 2.0 %shard_map.119 = (bf16[64,24,128]{2,1,0:T(8,128)(2,1)S(1)}, s32[1,1]{1,0:T(1,128)S(4)}) custom-call(s32[64,1,128]{2,1,0:T(1,128)S(1)} %all-to-all-done.1.asked_ref, bf16[48,4096]{1,0:T(8,128)(2,1)S(1)} %bitcast.14), custom_call_target="tpu_custom_call" | custom-call | flops 5368709120 | bytes 1048576 | tf_op jit(solution)/shard_map/pallas_call | solution.py:242
  39.4 17.4 %all_to_all.19.reply_ref = bf16[64,24,128]{2,1,0:T(8,128)(2,1)S(1)} all-to-all(bf16[64,24,128]{2,1,0:T(8,128)(2,1)S(1)} %get-tuple-element.22), channel_id=1, replica_groups=mesh['rows'=64,'feat'=16] {'rows'}, dimensions={0} | all-to-all | bytes 786432 | tf_op jit(solution)/shard_map/all_to_all | solution.py:358
  56.9 0.0 copy-start
  56.9 0.0 copy-start.1
  56.9 0.0 copy-start.2
  56.9 0.0 copy-start.3
  56.9 0.0 copy-start.4
  56.9 0.0 copy-start.5
  56.9 0.0 copy-start.6
  56.9 0.0 copy-start.7
  56.9 1.4 %shard_map.120 = bf16[256,128]{1,0:T(8,128)(2,1)S(1)} custom-call(bf16[64,24,128]{2,1,0:T(8,128)(2,1)S(1)} %all_to_all.19.reply_ref, f32[64,128]{1,0:T(8,128)S(1)} %get-tuple-element.23.code_ref, f32[512,128]{1,0:T(8,128)S(1)} %get-tuple-element.29.rest_ref), custom_call_target="tpu_custom_call" | custom-call | flops 4294967296 | bytes 1048576 | tf_op jit(solution)/shard_map/pallas_call | solution.py:242
  58.3 19.1 %all_to_all.20.part_ref = bf16[16,16,128]{2,1,0:T(8,128)(2,1)S(1)} all-to-all(bf16[16,16,128]{2,1,0:T(8,128)(2,1)S(1)} %bitcast.10), channel_id=1, replica_groups=mesh['rows'=64,'feat'=16] {'feat'}, dimensions={0} | all-to-all | bytes 131072 | tf_op jit(solution)/shard_map/all_to_all | solution.py:358
  77.4 0.0 copy-done
  77.4 0.0 copy-done.1
  77.4 0.0 copy-done.2
  77.4 0.0 copy-done.3
  77.4 0.0 copy-done.4
  77.4 0.0 copy-done.5
  77.4 0.0 copy-done.6
  77.5 0.0 copy-done.7
  77.5 1.9 %shard_map.121 = bf16[16,1024]{1,0:T(8,128)(2,1)} custom-call(bf16[16,16,128]{2,1,0:T(8,128)(2,1)S(1)} %all_to_all.20.part_ref, bf16[768,1024]{1,0:T(8,128)(2,1)S(1)} %copy-done.2, bf16[768,1024]{1,0:T(8,128)(2,1)S(1)} %copy-done.3, f32[1,1024]{1,0:T(1,128)S(1)} %bitcast.11, bf16[1024,1024]{1,0:T(8,128)(2,1)S(1)} %copy-done, ...), custom_call_target="tpu_custom_call" | custom-call | flops 3221225472 | bytes 1048576 | tf_op jit(solution)/shard_map/pallas_call | solution.py:242
  (2 shorter events, 0.1 us)
Async XLA Ops:
  0.0 37.4 %copy-start.8 = (bf16[4096,48]{0,1:T(8,128)(2,1)S(1)}, bf16[4096,48]{0,1:T(8,128)(2,1)}, u32[]{:S(2)}) copy-start(bf16[4096,48]{0,1:T(8,128)(2,1)} %param.14) | copy-start | bytes 1179652
  2.6 34.7 %all-to-all-start.1 = ((s32[64,1,128]{2,1,0:T(1,128)}), s32[64,1,128]{2,1,0:T(1,128)S(1)}, u32[]{:S(2)}, u32[]{:S(2)}) async-start(s32[64,1,128]{2,1,0:T(1,128)} %get-tuple-element.21), calls=%async_computation.1 | async-start | bytes 65536 | tf_op jit(solution)/shard_map/all_to_all | solution.py:358
  56.9 20.6 %copy-start = (bf16[1024,1024]{1,0:T(8,128)(2,1)S(1)}, bf16[1024,1024]{1,0:T(8,128)(2,1)}, u32[]{:S(2)}) copy-start(bf16[1024,1024]{1,0:T(8,128)(2,1)} %w2_self_ref.1) | copy-start | bytes 6291460
  56.9 20.6 %copy-start.1 = (bf16[1024,1024]{1,0:T(8,128)(2,1)S(1)}, bf16[1024,1024]{1,0:T(8,128)(2,1)}, u32[]{:S(2)}) copy-start(bf16[1024,1024]{1,0:T(8,128)(2,1)} %w2_neigh_ref.1) | copy-start | bytes 6291460
  56.9 20.6 %copy-start.2 = (bf16[768,1024]{1,0:T(8,128)(2,1)S(1)}, bf16[768,1024]{1,0:T(8,128)(2,1)}, u32[]{:S(2)}) copy-start(bf16[768,1024]{1,0:T(8,128)(2,1)} %w1_self_ref.1) | copy-start | bytes 4718596
  56.9 20.6 %copy-start.3 = (bf16[768,1024]{1,0:T(8,128)(2,1)S(1)}, bf16[768,1024]{1,0:T(8,128)(2,1)}, u32[]{:S(2)}) copy-start(bf16[768,1024]{1,0:T(8,128)(2,1)} %w1_neigh_ref.1) | copy-start | bytes 4718596
  56.9 20.6 %copy-start.4 = (s32[16,10]{1,0:T(8,128)S(1)}, s32[16,10]{1,0:T(8,128)}, u32[]{:S(2)}) copy-start(s32[16,10]{1,0:T(8,128)} %neighbours_ref.1) | copy-start | bytes 1924
  56.9 20.6 %copy-start.5 = (f32[1024]{0:T(1024)S(1)}, f32[1024]{0:T(1024)}, u32[]{:S(2)}) copy-start(f32[1024]{0:T(1024)} %param.17) | copy-start | bytes 12292
  56.9 20.6 %copy-start.6 = (f32[1024]{0:T(1024)S(1)}, f32[1024]{0:T(1024)}, u32[]{:S(2)}) copy-start(f32[1024]{0:T(1024)} %param.20) | copy-start | bytes 12292
  56.9 20.6 %copy-start.7 = (s32[16]{0:T(128)S(1)}, s32[16]{0:T(128)}, u32[]{:S(2)}) copy-start(s32[16]{0:T(128)} %param.25) | copy-start | bytes 196

commit v8 on v7

--- a/solution.py
+++ b/solution.py
@@ -128,7 +128,8 @@
     )
 
 
-def find_first_kernel(asked_ref, features_ref, found_ref, crowded_ref, table, scratch):
+def find_first_kernel(asked_ref, features_ref, found_ref, crowded_ref, none_ref, table, scratch):
+    none_ref[...] = jnp.zeros_like(none_ref)
     asked = asked_ref[:, 0, :]
     crowded_ref[0, 0] = jnp.max(jnp.where(iota(asked.shape, 1) == FLAG, asked, 0))
     find_kernel(asked_ref, features_ref, found_ref, table, scratch)
@@ -280,18 +281,19 @@
     ]
 
 
-def find_first(asked, features):
+def find_first(asked, features, targets):
     return call(
         find_first_kernel,
         [
             pltpu.VMEM((PEERS, PART, LANES), jnp.bfloat16),
             pltpu.SMEM((1, 1), jnp.int32),
+            jax.ShapeDtypeStruct((2 * targets, LANES), jnp.float32),
         ],
         find_scratch(),
         5 << 30,
         asked,
         features.T,
-        out_spaces=[VMEM, pltpu.SMEM],
+        out_spaces=[VMEM, pltpu.SMEM, VMEM],
     )
 
 
@@ -375,16 +377,16 @@
     targets = count_one.shape[0]
     requests, code = route(owner, row_index, count_one)
     asked = exchange(requests, "rows")
-    found, crowded = find_first(asked, features)
-
-    def more(asked, features, code):
+    found, crowded, none = find_first(asked, features, targets)
+
+    def more(asked, features, code, none):
         found = find(later_slots(asked), features)
         return rest_sums(exchange(found, "rows"), later_slots(code), targets)
 
-    def no_more(asked, features, code):
-        return jnp.zeros((2 * targets, LANES), jnp.float32)
-
-    rest = lax.cond(crowded[0, 0] > 0, more, no_more, asked, features, code)
+    def no_more(asked, features, code, none):
+        return none
+
+    rest = lax.cond(crowded[0, 0] > 0, more, no_more, asked, features, code, none)
     mine = means(exchange(found, "rows"), code, rest)
     parts = exchange(mine.reshape(-1, BLOCK, LANES), "feat")
     return layers(

time: 79.6 us -> 78.8 us (0.990)
  blocking collectives: 36.5 us -> 71.1 us
  starting transfers between devices: 24 us -> 0 us
  waiting for transfers between devices: 10.8 us -> 0 us
    all_to_all x2 -> x3, blocking collectives: 36.5 us -> 71.1 us  [exchange(): return lax.all_to_all(array, axis, split_axis=0, concat_axis=0, tiled=True)]
    all_to_all x1 -> x0, starting transfers between devices: 24 us -> none  [exchange(): return lax.all_to_all(array, axis, split_axis=0, concat_axis=0, tiled=True)]
    all_to_all x1 -> x0, waiting for transfers between devices: 10.8 us -> none  [exchange(): return lax.all_to_all(array, axis, split_axis=0, concat_axis=0, tiled=True)]
  transfers between devices with their start and end apart: 1 -> 0, of which waited for: 1 -> 0; matrix products, arithmetic and copies ran while one was open for 0% -> 0% of each run, Pallas kernels for 0% -> 0%
where the time goes in v8:
time: 78.8 us; the launch traced here: 78.5 us
  blocking collectives  71.1 us (90%)
  Pallas kernels  7.26 us (9%)
    all_to_all x3, blocking collectives, exchange(): return lax.all_to_all(array, axis, split_axis=0, concat_axis=0, tiled=True)  71.1 us
    pallas_call x4, Pallas kernels, call(): pl.pallas_call(kernel, out_shape=out_shape, in_specs=[pl.BlockSpec(memory...  7.26 us

profile of v8, /device:TPU:1, one launch (start us, length us, event | category | flops | bytes accessed | tf_op | source)
XLA Modules:
  0.0 78.5 jit_solution(16338997093338565735)
XLA Ops:
  0.0 0.0 copy-start.8
  0.0 2.0 %shard_map.118 = (s32[64,1,128]{2,1,0:T(1,128)S(1)}, f32[64,128]{1,0:T(8,128)S(1)}) custom-call(s32[32,128]{1,0:T(8,128)} %bitcast.16, s32[32,128]{1,0:T(8,128)} %bitcast.17, s32[2,128]{1,0:T(2,128)} %bitcast.18), custom_call_target="tpu_custom_call" | custom-call | flops 1073741824 | bytes 1048576 | tf_op jit(solution)/shard_map/pallas_call | solution.py:243
  2.0 34.6 %all_to_all.19.asked_ref = s32[64,1,128]{2,1,0:T(1,128)S(1)} all-to-all(s32[64,1,128]{2,1,0:T(1,128)S(1)} %get-tuple-element.23), channel_id=1, replica_groups=mesh['rows'=64,'feat'=16] {'rows'}, dimensions={0} | all-to-all | bytes 65536 | tf_op jit(solution)/shard_map/all_to_all | solution.py:360
  36.6 0.0 copy-done.8
  36.6 2.0 %shard_map.119 = (bf16[64,24,128]{2,1,0:T(8,128)(2,1)S(1)}, s32[1,1]{1,0:T(1,128)S(4)}, f32[512,128]{1,0:T(8,128)S(1)}) custom-call(s32[64,1,128]{2,1,0:T(1,128)S(1)} %all_to_all.19.asked_ref, bf16[48,4096]{1,0:T(8,128)(2,1)S(1)} %bitcast.14), custom_call_target="tpu_custom_call" | custom-call | flops 5368709120 | bytes 1048576 | tf_op jit(solution)/shard_map/pallas_call | solution.py:243
  38.6 17.4 %all_to_all.20.reply_ref = bf16[64,24,128]{2,1,0:T(8,128)(2,1)S(1)} all-to-all(bf16[64,24,128]{2,1,0:T(8,128)(2,1)S(1)} %get-tuple-element.24), channel_id=1, replica_groups=mesh['rows'=64,'feat'=16] {'rows'}, dimensions={0} | all-to-all | bytes 786432 | tf_op jit(solution)/shard_map/all_to_all | solution.py:360
  56.1 0.0 copy-start
  56.1 0.0 copy-start.1
  56.1 0.0 copy-start.2
  56.1 0.0 copy-start.3
  56.1 0.0 copy-start.4
  56.1 0.0 copy-start.5
  56.1 0.0 copy-start.6
  56.1 0.0 copy-start.7
  56.1 1.4 %shard_map.120 = bf16[256,128]{1,0:T(8,128)(2,1)S(1)} custom-call(bf16[64,24,128]{2,1,0:T(8,128)(2,1)S(1)} %all_to_all.20.reply_ref, f32[64,128]{1,0:T(8,128)S(1)} %get-tuple-element.25.code_ref, f32[512,128]{1,0:T(8,128)S(1)} %get-tuple-element.32.rest_ref), custom_call_target="tpu_custom_call" | custom-call | flops 4294967296 | bytes 1048576 | tf_op jit(solution)/shard_map/pallas_call | solution.py:243
  57.5 19.1 %all_to_all.21.part_ref = bf16[16,16,128]{2,1,0:T(8,128)(2,1)S(1)} all-to-all(bf16[16,16,128]{2,1,0:T(8,128)(2,1)S(1)} %bitcast.10), channel_id=1, replica_groups=mesh['rows'=64,'feat'=16] {'feat'}, dimensions={0} | all-to-all | bytes 131072 | tf_op jit(solution)/shard_map/all_to_all | solution.py:360
  76.6 0.0 copy-done
  76.6 0.0 copy-done.1
  76.6 0.0 copy-done.2
  76.6 0.0 copy-done.3
  76.6 0.0 copy-done.4
  76.6 0.0 copy-done.5
  76.7 0.0 copy-done.6
  76.7 0.0 copy-done.7
  76.7 1.9 %shard_map.121 = bf16[16,1024]{1,0:T(8,128)(2,1)} custom-call(bf16[16,16,128]{2,1,0:T(8,128)(2,1)S(1)} %all_to_all.21.part_ref, bf16[768,1024]{1,0:T(8,128)(2,1)S(1)} %copy-done.2, bf16[768,1024]{1,0:T(8,128)(2,1)S(1)} %copy-done.3, f32[1,1024]{1,0:T(1,128)S(1)} %bitcast.11, bf16[1024,1024]{1,0:T(8,128)(2,1)S(1)} %copy-done, ...), custom_call_target="tpu_custom_call" | custom-call | flops 3221225472 | bytes 1048576 | tf_op jit(solution)/shard_map/pallas_call | solution.py:243
  (1 shorter events, 0.0 us)
Async XLA Ops:
  0.0 36.6 %copy-start.8 = (bf16[4096,48]{0,1:T(8,128)(2,1)S(1)}, bf16[4096,48]{0,1:T(8,128)(2,1)}, u32[]{:S(2)}) copy-start(bf16[4096,48]{0,1:T(8,128)(2,1)} %param.14) | copy-start | bytes 1179652
  56.1 20.6 %copy-start = (bf16[1024,1024]{1,0:T(8,128)(2,1)S(1)}, bf16[1024,1024]{1,0:T(8,128)(2,1)}, u32[]{:S(2)}) copy-start(bf16[1024,1024]{1,0:T(8,128)(2,1)} %w2_self_ref.1) | copy-start | bytes 6291460
  56.1 20.6 %copy-start.1 = (bf16[1024,1024]{1,0:T(8,128)(2,1)S(1)}, bf16[1024,1024]{1,0:T(8,128)(2,1)}, u32[]{:S(2)}) copy-start(bf16[1024,1024]{1,0:T(8,128)(2,1)} %w2_neigh_ref.1) | copy-start | bytes 6291460
  56.1 20.6 %copy-start.2 = (bf16[768,1024]{1,0:T(8,128)(2,1)S(1)}, bf16[768,1024]{1,0:T(8,128)(2,1)}, u32[]{:S(2)}) copy-start(bf16[768,1024]{1,0:T(8,128)(2,1)} %w1_self_ref.1) | copy-start | bytes 4718596
  56.1 20.6 %copy-start.3 = (bf16[768,1024]{1,0:T(8,128)(2,1)S(1)}, bf16[768,1024]{1,0:T(8,128)(2,1)}, u32[]{:S(2)}) copy-start(bf16[768,1024]{1,0:T(8,128)(2,1)} %w1_neigh_ref.1) | copy-start | bytes 4718596
  56.1 20.6 %copy-start.4 = (s32[16,10]{1,0:T(8,128)S(1)}, s32[16,10]{1,0:T(8,128)}, u32[]{:S(2)}) copy-start(s32[16,10]{1,0:T(8,128)} %neighbours_ref.1) | copy-start | bytes 1924
  56.1 20.6 %copy-start.5 = (f32[1024]{0:T(1024)S(1)}, f32[1024]{0:T(1024)}, u32[]{:S(2)}) copy-start(f32[1024]{0:T(1024)} %param.17) | copy-start | bytes 12292
  56.1 20.6 %copy-start.6 = (f32[1024]{0:T(1024)S(1)}, f32[1024]{0:T(1024)}, u32[]{:S(2)}) copy-start(f32[1024]{0:T(1024)} %param.20) | copy-start | bytes 12292
  56.1 20.6 %copy-start.7 = (s32[16]{0:T(128)S(1)}, s32[16]{0:T(128)}, u32[]{:S(2)}) copy-start(s32[16]{0:T(128)} %param.25) | copy-start | bytes 196

commit v9 on v8

--- a/solution.py
+++ b/solution.py
@@ -164,20 +164,28 @@
 
 def sums_of(reply_ref, code_ref, scratch, targets):
     spread(code_ref[...], scratch)
-    row = iota((2 * targets, 2 * LANES), 0)
-    wanted = jnp.where(row < targets, -(row + 1), row - targets + 1)
-    wanted = wanted.astype(jnp.float32).astype(jnp.bfloat16)
+    number = iota((targets, 2 * LANES), 0).astype(jnp.float32).astype(jnp.bfloat16)
     one = jnp.bfloat16(1.0)
     zero = jnp.bfloat16(0.0)
     members, columns = [], []
     for peer in range(0, PEERS, 4):
         code = jnp.concatenate([two_peers(scratch, peer + 2 * h) for h in range(2)], axis=1)
-        members.append(jnp.where(wanted == code.astype(jnp.bfloat16), one, zero))
+        members.append(jnp.where(number == (jnp.abs(code) - 1.0).astype(jnp.bfloat16), one, zero))
+        own = jnp.where(code < 0.0, 1.0, 0.0).astype(jnp.bfloat16)
+        neigh = jnp.where(code > 0.0, 1.0, 0.0).astype(jnp.bfloat16)
         for h in range(2):
             tiles = [reply_ref[peer + 2 * h + x].astype(jnp.float32) for x in range(2)]
-            rows = [tile.astype(jnp.bfloat16) for tile in [jnp.concatenate(swap(*tiles), axis=0)]]
+            rows = jnp.concatenate(swap(*tiles), axis=0).astype(jnp.bfloat16)
+            lanes = slice(h * LANES, (h + 1) * LANES)
             columns.append(
-                jnp.concatenate(rows + rows + [jnp.ones((32, LANES), jnp.bfloat16)], axis=0)
+                jnp.concatenate(
+                    [
+                        rows * own[:, lanes],
+                        rows * neigh[:, lanes],
+                        jnp.broadcast_to(neigh[:, lanes], (LANES - 2 * WIDTH, LANES)),
+                    ],
+                    axis=0,
+                )
             )
     return lax.dot_general(
         jnp.concatenate(members, axis=1),
@@ -188,16 +196,13 @@
 
 
 def mean_kernel(reply_ref, code_ref, rest_ref, out_ref, scratch):
-    targets = out_ref.shape[0]
-    sums = sums_of(reply_ref, code_ref, scratch, targets) + rest_ref[...]
-    own = sums[:targets]
-    neigh = sums[targets:]
-    mean = neigh / neigh[:, 2 * WIDTH : 2 * WIDTH + 1]
-    out_ref[...] = jnp.where(iota(own.shape, 1) < WIDTH, own, mean).astype(jnp.bfloat16)
+    sums = sums_of(reply_ref, code_ref, scratch, out_ref.shape[0]) + rest_ref[...]
+    mean = sums / sums[:, 2 * WIDTH : 2 * WIDTH + 1]
+    out_ref[...] = jnp.where(iota(sums.shape, 1) < WIDTH, sums, mean).astype(jnp.bfloat16)
 
 
 def rest_kernel(reply_ref, code_ref, sums_ref, scratch):
-    sums_ref[...] = sums_of(reply_ref, code_ref, scratch, sums_ref.shape[0] // 2)
+    sums_ref[...] = sums_of(reply_ref, code_ref, scratch, sums_ref.shape[0])
 
 
 def layers_kernel(
@@ -287,7 +292,7 @@
         [
             pltpu.VMEM((PEERS, PART, LANES), jnp.bfloat16),
             pltpu.SMEM((1, 1), jnp.int32),
-            jax.ShapeDtypeStruct((2 * targets, LANES), jnp.float32),
+            jax.ShapeDtypeStruct((targets, LANES), jnp.float32),
         ],
         find_scratch(),
         5 << 30,
@@ -311,7 +316,7 @@
 def means(replies, code, rest):
     return call(
         mean_kernel,
-        [jax.ShapeDtypeStruct((rest.shape[0] // 2, LANES), jnp.bfloat16)],
+        [jax.ShapeDtypeStruct(rest.shape, jnp.bfloat16)],
         [pltpu.VMEM((PEERS, LANES), jnp.float32)],
         4 << 30,
         replies,
@@ -323,7 +328,7 @@
 def rest_sums(replies, code, targets):
     return call(
         rest_kernel,
-        [jax.ShapeDtypeStruct((2 * targets, LANES), jnp.float32)],
+        [jax.ShapeDtypeStruct((targets, LANES), jnp.float32)],
         [pltpu.VMEM((PEERS, LANES), jnp.float32)],
         4 << 30,
         replies,

time: 78.8 us -> 78.4 us (level)
  no operation moved by 1% of the time
where the time goes in v9:
time: 78.4 us; the launch traced here: 78.2 us
  blocking collectives  71.3 us (91%)
  Pallas kernels  6.73 us (9%)
    all_to_all x3, blocking collectives, exchange(): return lax.all_to_all(array, axis, split_axis=0, concat_axis=0, tiled=True)  71.3 us
    pallas_call x4, Pallas kernels, call(): pl.pallas_call(kernel, out_shape=out_shape, in_specs=[pl.BlockSpec(memory...  6.73 us

profile of v9, /device:TPU:1, one launch (start us, length us, event | category | flops | bytes accessed | tf_op | source)
XLA Modules:
  0.0 78.2 jit_solution(16343833503447888617)
XLA Ops:
  0.0 0.0 copy-start.8
  0.0 2.0 %shard_map.118 = (s32[64,1,128]{2,1,0:T(1,128)S(1)}, f32[64,128]{1,0:T(8,128)S(1)}) custom-call(s32[32,128]{1,0:T(8,128)} %bitcast.16, s32[32,128]{1,0:T(8,128)} %bitcast.17, s32[2,128]{1,0:T(2,128)} %bitcast.18), custom_call_target="tpu_custom_call" | custom-call | flops 1073741824 | bytes 1048576 | tf_op jit(solution)/shard_map/pallas_call | solution.py:248
  2.0 34.6 %all_to_all.19.asked_ref = s32[64,1,128]{2,1,0:T(1,128)S(1)} all-to-all(s32[64,1,128]{2,1,0:T(1,128)S(1)} %get-tuple-element.23), channel_id=1, replica_groups=mesh['rows'=64,'feat'=16] {'rows'}, dimensions={0} | all-to-all | bytes 65536 | tf_op jit(solution)/shard_map/all_to_all | solution.py:365
  36.6 0.0 copy-done.8
  36.6 2.0 %shard_map.119 = (bf16[64,24,128]{2,1,0:T(8,128)(2,1)S(1)}, s32[1,1]{1,0:T(1,128)S(4)}, f32[256,128]{1,0:T(8,128)S(1)}) custom-call(s32[64,1,128]{2,1,0:T(1,128)S(1)} %all_to_all.19.asked_ref, bf16[48,4096]{1,0:T(8,128)(2,1)S(1)} %bitcast.14), custom_call_target="tpu_custom_call" | custom-call | flops 5368709120 | bytes 1048576 | tf_op jit(solution)/shard_map/pallas_call | solution.py:248
  38.6 17.4 %all_to_all.20.reply_ref = bf16[64,24,128]{2,1,0:T(8,128)(2,1)S(1)} all-to-all(bf16[64,24,128]{2,1,0:T(8,128)(2,1)S(1)} %get-tuple-element.24), channel_id=1, replica_groups=mesh['rows'=64,'feat'=16] {'rows'}, dimensions={0} | all-to-all | bytes 786432 | tf_op jit(solution)/shard_map/all_to_all | solution.py:365
  56.1 0.0 copy-start
  56.1 0.0 copy-start.1
  56.1 0.0 copy-start.2
  56.1 0.0 copy-start.3
  56.1 0.0 copy-start.4
  56.1 0.0 copy-start.5
  56.1 0.0 copy-start.6
  56.1 0.0 copy-start.7
  56.1 0.9 %shard_map.120 = bf16[256,128]{1,0:T(8,128)(2,1)S(1)} custom-call(bf16[64,24,128]{2,1,0:T(8,128)(2,1)S(1)} %all_to_all.20.reply_ref, f32[64,128]{1,0:T(8,128)S(1)} %get-tuple-element.25.code_ref, f32[256,128]{1,0:T(8,128)S(1)} %get-tuple-element.32.rest_ref), custom_call_target="tpu_custom_call" | custom-call | flops 4294967296 | bytes 1048576 | tf_op jit(solution)/shard_map/pallas_call | solution.py:248
  57.0 19.2 %all_to_all.21.part_ref = bf16[16,16,128]{2,1,0:T(8,128)(2,1)S(1)} all-to-all(bf16[16,16,128]{2,1,0:T(8,128)(2,1)S(1)} %bitcast.10), channel_id=1, replica_groups=mesh['rows'=64,'feat'=16] {'feat'}, dimensions={0} | all-to-all | bytes 131072 | tf_op jit(solution)/shard_map/all_to_all | solution.py:365
  76.2 0.0 copy-done
  76.2 0.0 copy-done.1
  76.2 0.0 copy-done.2
  76.2 0.0 copy-done.3
  76.2 0.0 copy-done.4
  76.3 0.0 copy-done.5
  76.3 0.0 copy-done.6
  76.3 0.0 copy-done.7
  76.3 1.9 %shard_map.121 = bf16[16,1024]{1,0:T(8,128)(2,1)} custom-call(bf16[16,16,128]{2,1,0:T(8,128)(2,1)S(1)} %all_to_all.21.part_ref, bf16[768,1024]{1,0:T(8,128)(2,1)S(1)} %copy-done.2, bf16[768,1024]{1,0:T(8,128)(2,1)S(1)} %copy-done.3, f32[1,1024]{1,0:T(1,128)S(1)} %bitcast.11, bf16[1024,1024]{1,0:T(8,128)(2,1)S(1)} %copy-done, ...), custom_call_target="tpu_custom_call" | custom-call | flops 3221225472 | bytes 1048576 | tf_op jit(solution)/shard_map/pallas_call | solution.py:248
  (1 shorter events, 0.0 us)
Async XLA Ops:
  0.0 36.6 %copy-start.8 = (bf16[4096,48]{0,1:T(8,128)(2,1)S(1)}, bf16[4096,48]{0,1:T(8,128)(2,1)}, u32[]{:S(2)}) copy-start(bf16[4096,48]{0,1:T(8,128)(2,1)} %param.14) | copy-start | bytes 1179652
  56.1 20.2 %copy-start = (bf16[1024,1024]{1,0:T(8,128)(2,1)S(1)}, bf16[1024,1024]{1,0:T(8,128)(2,1)}, u32[]{:S(2)}) copy-start(bf16[1024,1024]{1,0:T(8,128)(2,1)} %w2_self_ref.1) | copy-start | bytes 6291460
  56.1 20.2 %copy-start.1 = (bf16[1024,1024]{1,0:T(8,128)(2,1)S(1)}, bf16[1024,1024]{1,0:T(8,128)(2,1)}, u32[]{:S(2)}) copy-start(bf16[1024,1024]{1,0:T(8,128)(2,1)} %w2_neigh_ref.1) | copy-start | bytes 6291460
  56.1 20.2 %copy-start.2 = (bf16[768,1024]{1,0:T(8,128)(2,1)S(1)}, bf16[768,1024]{1,0:T(8,128)(2,1)}, u32[]{:S(2)}) copy-start(bf16[768,1024]{1,0:T(8,128)(2,1)} %w1_self_ref.1) | copy-start | bytes 4718596
  56.1 20.2 %copy-start.3 = (bf16[768,1024]{1,0:T(8,128)(2,1)S(1)}, bf16[768,1024]{1,0:T(8,128)(2,1)}, u32[]{:S(2)}) copy-start(bf16[768,1024]{1,0:T(8,128)(2,1)} %w1_neigh_ref.1) | copy-start | bytes 4718596
  56.1 20.2 %copy-start.4 = (s32[16,10]{1,0:T(8,128)S(1)}, s32[16,10]{1,0:T(8,128)}, u32[]{:S(2)}) copy-start(s32[16,10]{1,0:T(8,128)} %neighbours_ref.1) | copy-start | bytes 1924
  56.1 20.2 %copy-start.5 = (f32[1024]{0:T(1024)S(1)}, f32[1024]{0:T(1024)}, u32[]{:S(2)}) copy-start(f32[1024]{0:T(1024)} %param.17) | copy-start | bytes 12292
  56.1 20.2 %copy-start.6 = (f32[1024]{0:T(1024)S(1)}, f32[1024]{0:T(1024)}, u32[]{:S(2)}) copy-start(f32[1024]{0:T(1024)} %param.20) | copy-start | bytes 12292
  56.1 20.2 %copy-start.7 = (s32[16]{0:T(128)S(1)}, s32[16]{0:T(128)}, u32[]{:S(2)}) copy-start(s32[16]{0:T(128)} %param.25) | copy-start | bytes 196

commit v10 on v9

--- a/solution.py
+++ b/solution.py
@@ -36,37 +36,38 @@
             ((owner_hbm, owner_ref), (row_hbm, row_ref), (count_hbm, count_ref))
         )
     ]
-    for copy in copies:
+    for copy in reversed(copies):
         copy.start()
-    for copy in copies:
-        copy.wait()
     chunks = owner_ref.shape[0]
     per_chunk = LANES // (K1 + 1)
     half = chunks // 2
     chunk = iota((chunks, LANES), 0)
     lane = iota((chunks, LANES), 1)
+    place = lane % (K1 + 1)
+    target = (chunk * per_chunk + lane // (K1 + 1) + 1).astype(jnp.float32)
+    pick = jnp.where(
+        iota((LANES, LANES), 0) % per_chunk == iota((LANES, LANES), 1) // (K1 + 1), 1.0, 0.0
+    ).astype(jnp.bfloat16)
+    before = iota((LANES, 2 * LANES), 0)
+    upto = iota((LANES, 2 * LANES), 1)
+    prefix = jnp.where((before < upto) | (upto >= LANES), 1.0, 0.0).astype(jnp.bfloat16)
+    code_ref[...] = jnp.zeros_like(code_ref)
+    copies[2].wait()
+
     count = count_ref[...].astype(jnp.float32)
     spread = jnp.concatenate(
         [jnp.broadcast_to(count[i : i + 1], (half, LANES)) for i in range(2)], axis=0
     )
     spread = jnp.where(lane // per_chunk == chunk % half, spread, 0.0)
-    pick = jnp.where(
-        iota((LANES, LANES), 0) % per_chunk == iota((LANES, LANES), 1) // (K1 + 1), 1.0, 0.0
-    )
-    limit = jnp.dot(
-        spread.astype(jnp.bfloat16), pick.astype(jnp.bfloat16), preferred_element_type=jnp.float32
-    )
-    place = lane % (K1 + 1)
-    target = (chunk * per_chunk + lane // (K1 + 1) + 1).astype(jnp.float32)
+    limit = jnp.dot(spread.astype(jnp.bfloat16), pick, preferred_element_type=jnp.float32)
     code = jnp.where(
         place == 0, -target, jnp.where(place.astype(jnp.float32) <= limit, target, 0.0)
     )
+    copies[0].wait()
+    copies[1].wait()
     owner = jnp.where(code == 0.0, -1, owner_ref[...])
     mask = owner[:, None, :] == iota((chunks, PEERS, LANES), 1)
     ones = jnp.where(mask, 1.0, 0.0)
-    before = iota((LANES, 2 * LANES), 0)
-    upto = iota((LANES, 2 * LANES), 1)
-    prefix = jnp.where((before < upto) | (upto >= LANES), 1.0, 0.0).astype(jnp.bfloat16)
     sums = jnp.dot(
         ones.astype(jnp.bfloat16).reshape(chunks * PEERS, LANES),
         prefix,
@@ -103,7 +104,6 @@
             values, slots = [], []
     crowded = jnp.where(jnp.max(offset) > USUAL, 1, 0)
     request_ref[...] = jnp.where(iota(request_ref.shape, 2) == FLAG, crowded, 0)
-    code_ref[...] = jnp.zeros_like(code_ref)
     request_ref[:, 0, :CAPACITY] = (
         total[:PEERS] * 64.0 + total[PEERS : 2 * PEERS]
     ).astype(jnp.int32)

time: 78.4 us -> 78.3 us (level)
  no operation moved by 1% of the time
where the time goes in v10:
time: 78.3 us; the launch traced here: 78.1 us
  blocking collectives  71.2 us (91%)
  Pallas kernels  6.69 us (9%)
    all_to_all x3, blocking collectives, exchange(): return lax.all_to_all(array, axis, split_axis=0, concat_axis=0, tiled=True)  71.2 us
    pallas_call x4, Pallas kernels, call(): pl.pallas_call(kernel, out_shape=out_shape, in_specs=[pl.BlockSpec(memory...  6.69 us

profile of v10, /device:TPU:1, one launch (start us, length us, event | category | flops | bytes accessed | tf_op | source)
XLA Modules:
  0.0 78.1 jit_solution(9517260767874238214)
XLA Ops:
  0.0 0.0 copy-start.8
  0.0 2.0 %shard_map.118 = (s32[64,1,128]{2,1,0:T(1,128)S(1)}, f32[64,128]{1,0:T(8,128)S(1)}) custom-call(s32[32,128]{1,0:T(8,128)} %bitcast.16, s32[32,128]{1,0:T(8,128)} %bitcast.17, s32[2,128]{1,0:T(2,128)} %bitcast.18), custom_call_target="tpu_custom_call" | custom-call | flops 1073741824 | bytes 1048576 | tf_op jit(solution)/shard_map/pallas_call | solution.py:248
  2.0 34.6 %all_to_all.19.asked_ref = s32[64,1,128]{2,1,0:T(1,128)S(1)} all-to-all(s32[64,1,128]{2,1,0:T(1,128)S(1)} %get-tuple-element.23), channel_id=1, replica_groups=mesh['rows'=64,'feat'=16] {'rows'}, dimensions={0} | all-to-all | bytes 65536 | tf_op jit(solution)/shard_map/all_to_all | solution.py:365
  36.6 0.0 copy-done.8
  36.6 2.0 %shard_map.119 = (bf16[64,24,128]{2,1,0:T(8,128)(2,1)S(1)}, s32[1,1]{1,0:T(1,128)S(4)}, f32[256,128]{1,0:T(8,128)S(1)}) custom-call(s32[64,1,128]{2,1,0:T(1,128)S(1)} %all_to_all.19.asked_ref, bf16[48,4096]{1,0:T(8,128)(2,1)S(1)} %bitcast.14), custom_call_target="tpu_custom_call" | custom-call | flops 5368709120 | bytes 1048576 | tf_op jit(solution)/shard_map/pallas_call | solution.py:248
  38.6 17.4 %all_to_all.20.reply_ref = bf16[64,24,128]{2,1,0:T(8,128)(2,1)S(1)} all-to-all(bf16[64,24,128]{2,1,0:T(8,128)(2,1)S(1)} %get-tuple-element.24), channel_id=1, replica_groups=mesh['rows'=64,'feat'=16] {'rows'}, dimensions={0} | all-to-all | bytes 786432 | tf_op jit(solution)/shard_map/all_to_all | solution.py:365
  56.0 0.0 copy-start
  56.0 0.0 copy-start.1
  56.0 0.0 copy-start.2
  56.0 0.0 copy-start.3
  56.0 0.0 copy-start.4
  56.0 0.0 copy-start.5
  56.1 0.0 copy-start.6
  56.1 0.0 copy-start.7
  56.1 0.9 %shard_map.120 = bf16[256,128]{1,0:T(8,128)(2,1)S(1)} custom-call(bf16[64,24,128]{2,1,0:T(8,128)(2,1)S(1)} %all_to_all.20.reply_ref, f32[64,128]{1,0:T(8,128)S(1)} %get-tuple-element.25.code_ref, f32[256,128]{1,0:T(8,128)S(1)} %get-tuple-element.32.rest_ref), custom_call_target="tpu_custom_call" | custom-call | flops 4294967296 | bytes 1048576 | tf_op jit(solution)/shard_map/pallas_call | solution.py:248
  57.0 19.2 %all_to_all.21.part_ref = bf16[16,16,128]{2,1,0:T(8,128)(2,1)S(1)} all-to-all(bf16[16,16,128]{2,1,0:T(8,128)(2,1)S(1)} %bitcast.10), channel_id=1, replica_groups=mesh['rows'=64,'feat'=16] {'feat'}, dimensions={0} | all-to-all | bytes 131072 | tf_op jit(solution)/shard_map/all_to_all | solution.py:365
  76.2 0.0 copy-done
  76.2 0.0 copy-done.1
  76.2 0.0 copy-done.2
  76.2 0.0 copy-done.3
  76.2 0.0 copy-done.4
  76.2 0.0 copy-done.5
  76.2 0.0 copy-done.6
  76.2 0.0 copy-done.7
  76.2 1.9 %shard_map.121 = bf16[16,1024]{1,0:T(8,128)(2,1)} custom-call(bf16[16,16,128]{2,1,0:T(8,128)(2,1)S(1)} %all_to_all.21.part_ref, bf16[768,1024]{1,0:T(8,128)(2,1)S(1)} %copy-done.2, bf16[768,1024]{1,0:T(8,128)(2,1)S(1)} %copy-done.3, f32[1,1024]{1,0:T(1,128)S(1)} %bitcast.11, bf16[1024,1024]{1,0:T(8,128)(2,1)S(1)} %copy-done, ...), custom_call_target="tpu_custom_call" | custom-call | flops 3221225472 | bytes 1048576 | tf_op jit(solution)/shard_map/pallas_call | solution.py:248
  (1 shorter events, 0.0 us)
Async XLA Ops:
  0.0 36.6 %copy-start.8 = (bf16[4096,48]{0,1:T(8,128)(2,1)S(1)}, bf16[4096,48]{0,1:T(8,128)(2,1)}, u32[]{:S(2)}) copy-start(bf16[4096,48]{0,1:T(8,128)(2,1)} %param.14) | copy-start | bytes 1179652
  56.0 20.2 %copy-start = (bf16[1024,1024]{1,0:T(8,128)(2,1)S(1)}, bf16[1024,1024]{1,0:T(8,128)(2,1)}, u32[]{:S(2)}) copy-start(bf16[1024,1024]{1,0:T(8,128)(2,1)} %w2_self_ref.1) | copy-start | bytes 6291460
  56.0 20.2 %copy-start.1 = (bf16[1024,1024]{1,0:T(8,128)(2,1)S(1)}, bf16[1024,1024]{1,0:T(8,128)(2,1)}, u32[]{:S(2)}) copy-start(bf16[1024,1024]{1,0:T(8,128)(2,1)} %w2_neigh_ref.1) | copy-start | bytes 6291460
  56.0 20.2 %copy-start.2 = (bf16[768,1024]{1,0:T(8,128)(2,1)S(1)}, bf16[768,1024]{1,0:T(8,128)(2,1)}, u32[]{:S(2)}) copy-start(bf16[768,1024]{1,0:T(8,128)(2,1)} %w1_self_ref.1) | copy-start | bytes 4718596
  56.0 20.2 %copy-start.3 = (bf16[768,1024]{1,0:T(8,128)(2,1)S(1)}, bf16[768,1024]{1,0:T(8,128)(2,1)}, u32[]{:S(2)}) copy-start(bf16[768,1024]{1,0:T(8,128)(2,1)} %w1_neigh_ref.1) | copy-start | bytes 4718596
  56.0 20.2 %copy-start.4 = (s32[16,10]{1,0:T(8,128)S(1)}, s32[16,10]{1,0:T(8,128)}, u32[]{:S(2)}) copy-start(s32[16,10]{1,0:T(8,128)} %neighbours_ref.1) | copy-start | bytes 1924
  56.0 20.2 %copy-start.5 = (f32[1024]{0:T(1024)S(1)}, f32[1024]{0:T(1024)}, u32[]{:S(2)}) copy-start(f32[1024]{0:T(1024)} %param.17) | copy-start | bytes 12292
  56.1 20.2 %copy-start.6 = (f32[1024]{0:T(1024)S(1)}, f32[1024]{0:T(1024)}, u32[]{:S(2)}) copy-start(f32[1024]{0:T(1024)} %param.20) | copy-start | bytes 12292
  56.1 20.2 %copy-start.7 = (s32[16]{0:T(128)S(1)}, s32[16]{0:T(128)}, u32[]{:S(2)}) copy-start(s32[16]{0:T(128)} %param.25) | copy-start | bytes 196
